TPU v7x, 256 devices: a whole 4x4x8 slice. The times are simulated.
256 devices in a mesh: dp: 64 (over z, y, x_hi), fsdp: 4 (over x_lo, core).
Axes of the slice: x: 4 (x_hi: 2, x_lo: 2; x = x_hi * 2 + x_lo), y: 4, z: 8, core: 2. Of those that a mesh axis runs over, the one named last changes fastest.
Arguments:
- image_features: float32 [8192, 1152], P(('dp', 'fsdp')), may hold values from -1.5 to 1.5
- text_features: float32 [8192, 1152], P(('dp', 'fsdp')), may hold values from -1.5 to 1.5
- image_proj: float32 [1152, 1152], P(None, 'fsdp'), may hold values from -0.1875 to 0.1875
- text_proj: float32 [1152, 1152], P(None, 'fsdp'), may hold values from -0.1875 to 0.1875
Outputs:
- grad_image_features: float32 [8192, 1152], P(('dp', 'fsdp'))
- grad_text_features: float32 [8192, 1152], P(('dp', 'fsdp'))
- grad_image_proj: float32 [1152, 1152], P(None, 'fsdp')
- grad_text_proj: float32 [1152, 1152], P(None, 'fsdp')
All inputs are finite; a program needn't handle non-finite values.
Results may differ from a plain program's by a relative error of at most 0.0003.
Values sent between devices are 32-bit elements; how exact they have to be, the bound alone decides.
A program may use at most 64 MiB of HBM per device.

v0:
```python
import jax
import jax.numpy as jnp
from jax import lax
from jax.sharding import PartitionSpec as P

logit_scale = 100.0
logit_bias = -10.0
epsilon_norm = 1e-06


def shifted(block, axis, distance):
    devices = range(lax.axis_size(axis))
    route = [((i - distance) % len(devices), i) for i in devices]
    return lax.ppermute(block, axis, route)


def normalize(values):
    inverse = lax.rsqrt(jnp.sum(values * values, axis=1, keepdims=True) + epsilon_norm)
    return (values * inverse, inverse)


def on_device(image_features, text_features, image_proj, text_proj):
    highest = lax.Precision.HIGHEST
    group_image, group_text = (
        lax.all_gather(image_features, "fsdp", axis=0, tiled=True),
        lax.all_gather(text_features, "fsdp", axis=0, tiled=True),
    )
    image_cols = jnp.dot(
        group_image, image_proj, precision=highest, preferred_element_type=jnp.float32
    )
    text_cols = jnp.dot(
        group_text, text_proj, precision=highest, preferred_element_type=jnp.float32
    )
    image_raw, text_raw = (
        lax.all_to_all(image_cols, "fsdp", split_axis=0, concat_axis=1, tiled=True),
        lax.all_to_all(text_cols, "fsdp", split_axis=0, concat_axis=1, tiled=True),
    )
    image_unit, image_inverse = normalize(image_raw)
    text_unit, text_inverse = normalize(text_raw)
    group_unit, group_inverse = (
        lax.all_gather(image_unit, "fsdp", axis=0, tiled=True),
        lax.all_gather(image_inverse, "fsdp", axis=0, tiled=True),
    )
    row_count = text_unit.shape[0]
    group_rows = group_unit.shape[0]
    group_count = lax.axis_size("dp")
    fsdp_index = lax.axis_index("fsdp")
    targets = (
        lax.broadcasted_iota(jnp.int32, (group_rows, row_count), 0)
        == lax.broadcasted_iota(jnp.int32, (group_rows, row_count), 1) + fsdp_index * row_count
    ).astype(jnp.float32)

    def contribute(text_block, target_mask):
        logits = (
            logit_scale
            * jnp.dot(
                group_unit, text_block.T, precision=highest, preferred_element_type=jnp.float32
            )
            + logit_bias
        )
        pair_grad = jax.nn.sigmoid(logits) - target_mask
        image_term = logit_scale * jnp.dot(
            pair_grad, text_block, precision=highest, preferred_element_type=jnp.float32
        )
        text_term = logit_scale * jnp.dot(
            pair_grad.T, group_unit, precision=highest, preferred_element_type=jnp.float32
        )
        return (image_term, text_term)

    image_zero = jnp.zeros(group_unit.shape, jnp.float32)

    def single_turn(turn_index, state_tuple):
        text_block, text_sums, image_sums = state_tuple
        opening = (turn_index == 0).astype(jnp.float32)
        image_term, text_term = contribute(text_block, targets * opening)
        text_block, text_sums = shifted((text_block, text_sums + text_term), "dp", 1)
        return (text_block, text_sums, image_sums + image_term)

    state_tuple = (text_unit, jnp.zeros(text_unit.shape, jnp.float32), image_zero)
    unused_block, text_grad, image_total = lax.fori_loop(0, group_count, single_turn, state_tuple)
    text_dz = text_inverse * (
        text_grad - text_unit * jnp.sum(text_unit * text_grad, axis=1, keepdims=True)
    )
    image_grad = lax.psum_scatter(image_total, "fsdp", scatter_dimension=0, tiled=True)
    image_dz = image_inverse * (
        image_grad - image_unit * jnp.sum(image_unit * image_grad, axis=1, keepdims=True)
    )
    image_dcols, text_dcols = (
        lax.all_to_all(image_dz, "fsdp", split_axis=1, concat_axis=0, tiled=True),
        lax.all_to_all(text_dz, "fsdp", split_axis=1, concat_axis=0, tiled=True),
    )
    feature_width = image_features.shape[1]
    image_part = jnp.dot(
        image_dcols, image_proj.T, precision=highest, preferred_element_type=jnp.float32
    )
    text_part = jnp.dot(
        text_dcols, text_proj.T, precision=highest, preferred_element_type=jnp.float32
    )
    combined = lax.psum_scatter(
        jnp.concatenate([image_part, text_part], axis=1), "fsdp", scatter_dimension=0, tiled=True
    )
    grad_image_features = combined[:, :feature_width]
    grad_text_features = combined[:, feature_width:]
    image_weight = jnp.dot(
        group_image.T, image_dcols, precision=highest, preferred_element_type=jnp.float32
    )
    text_weight = jnp.dot(
        group_text.T, text_dcols, precision=highest, preferred_element_type=jnp.float32
    )
    grad_image_proj, grad_text_proj = lax.psum((image_weight, text_weight), "dp")
    return (grad_image_features, grad_text_features, grad_image_proj, grad_text_proj)


def solution(mesh):
    placed = (P(("dp", "fsdp"), None), P(("dp", "fsdp"), None), P(None, "fsdp"), P(None, "fsdp"))
    return jax.shard_map(
        on_device,
        mesh=mesh,
        in_specs=placed,
        out_specs=(
            P(("dp", "fsdp"), None),
            P(("dp", "fsdp"), None),
            P(None, "fsdp"),
            P(None, "fsdp"),
        ),
        check_vma=False,
    )
```

profile of v0, /device:TPU:8, one launch (start us, length us, event | category | flops | bytes accessed | tf_op | source)
XLA Modules:
  0.0 1721.8 jit_solution(2988270321710785547)
XLA Ops:
  49.8 896.1 %while.18 = (s32[]{:T(128)}, f32[32,1152]{1,0:T(8,128)S(1)}, f32[32,1152]{1,0:T(8,128)S(1)}, f32[128,1152]{1,0:T(8,128)S(1)}, f32[128,1152]{1,0:T(8,128)S(1)}, /*index=5*/s32[32]{0:T(128)}, s32[]{:T(128)}, s32[]{:T(128)}) while((s32[]{:T(128)}, f32[32,1152]{1,0:T(8,128)S(1)}, f32[32,1152]{1,0:T(8,128)S(1)}, ...), condition=%wide.region_3.0_spmd.clone, body=%wide.region_2.0_spmd.clone.sunk | while | flops 170418176 | bytes 4473144 | solution.py:80
  186.7 10.7 collective-permute-done.1
  200.8 10.7 collective-permute-done.1
  214.9 10.7 collective-permute-done.1
  229.1 10.7 collective-permute-done.1
  243.2 10.7 collective-permute-done.1
  257.3 10.8 collective-permute-done.1
  285.5 10.7 collective-permute-done.1
  327.9 10.7 collective-permute-done.1
  342.0 10.7 collective-permute-done.1
  356.2 10.7 collective-permute-done.1
  370.3 10.7 collective-permute-done.1
  384.4 10.7 collective-permute-done.1
  398.5 10.7 collective-permute-done.1
  412.6 10.7 collective-permute-done.1
  426.8 10.7 collective-permute-done.1
  440.9 10.7 collective-permute-done.1
  455.0 10.7 collective-permute-done.1
  469.1 10.7 collective-permute-done.1
  483.3 10.8 collective-permute-done.1
  511.5 10.7 collective-permute-done.1
  553.9 10.7 collective-permute-done.1
  568.0 10.7 collective-permute-done.1
  582.1 10.7 collective-permute-done.1
  596.2 10.7 collective-permute-done.1
  610.4 10.7 collective-permute-done.1
  624.5 10.7 collective-permute-done.1
  638.6 10.7 collective-permute-done.1
  652.7 10.7 collective-permute-done.1
  666.9 10.7 collective-permute-done.1
  681.0 10.7 collective-permute-done.1
  695.1 10.7 collective-permute-done.1
  709.2 10.8 collective-permute-done.1
  737.5 10.7 collective-permute-done.1
  794.0 10.7 collective-permute-done.1
  808.1 10.7 collective-permute-done.1
  822.2 10.7 collective-permute-done.1
  836.3 10.7 collective-permute-done.1
  850.5 10.7 collective-permute-done.1
  864.6 10.7 collective-permute-done.1
  878.7 10.7 collective-permute-done.1
  892.8 10.7 collective-permute-done.1
  906.9 10.7 collective-permute-done.1
  921.1 10.7 collective-permute-done.1
  935.2 10.8 collective-permute-done.1
  953.1 23.4 %reduce-scatter.3.cloned.1.call-done = f32[32,1152]{1,0:T(8,128)} async-done(((f32[128,1152]{1,0:T(8,128)}), f32[32,1152]{1,0:T(8,128)}) %reduce-scatter.3.cloned.1.call-update) | async-done | bytes 147472 | tf_op jit(solution)/shard_map/reduce_scatter | solution.py:84
  998.3 18.7 %reduce-scatter.5.cloned.1.call-done = f32[32,2304]{1,0:T(8,128)} async-done(((f32[128,2304]{1,0:T(8,128)}), f32[32,2304]{1,0:T(8,128)}) %reduce-scatter.5.cloned.1.call-update) | async-done | bytes 294928 | tf_op jit(solution)/shard_map/reduce_scatter | solution.py:99
  1018.7 692.9 %all-reduce.3.cloned.1.call-done = (f32[1152,288]{0,1:T(8,128)}, f32[1152,288]{0,1:T(8,128)}) async-done(((f32[1152,288]{0,1:T(8,128)}, f32[1152,288]{0,1:T(8,128)}), (f32[1152,288]{0,1:T(8,128)}, f32[1152,288]{0,1:T(8,128)})) %all-reduce.3.cloned.1.call-update) | async-done | bytes 2654224 | tf_op jit(solution)/shard_map/psum | solution.py:110
  (544 shorter events, 497.7 us)
Async XLA Ops:
  18.8 15.6 all-to-all-start
  37.8 938.8 %reduce-scatter.3.cloned.1.call-start = ((), (), s32[]{:S(2)}) async-start(), calls=%async_computation.6 | async-start | bytes 737280 | tf_op jit(solution)/shard_map/reduce_scatter | solution.py:84
  112.7 14.1 collective-permute-start
  126.8 14.1 collective-permute-start
  141.0 14.1 collective-permute-start
  155.1 14.1 collective-permute-start
  169.2 14.1 collective-permute-start
  183.3 14.1 collective-permute-start
  197.5 14.1 collective-permute-start
  211.6 14.1 collective-permute-start
  225.7 14.1 collective-permute-start
  239.8 14.1 collective-permute-start
  253.9 14.1 collective-permute-start
  268.1 14.1 collective-permute-start
  282.2 14.1 collective-permute-start
  296.3 14.1 collective-permute-start
  310.4 14.1 collective-permute-start
  324.6 14.1 collective-permute-start
  338.7 14.1 collective-permute-start
  352.8 14.1 collective-permute-start
  366.9 14.1 collective-permute-start
  381.0 14.1 collective-permute-start
  395.2 14.1 collective-permute-start
  409.3 14.1 collective-permute-start
  423.4 14.1 collective-permute-start
  437.5 14.1 collective-permute-start
  451.7 14.1 collective-permute-start
  465.8 14.1 collective-permute-start
  479.9 14.1 collective-permute-start
  494.0 14.1 collective-permute-start
  508.1 14.1 collective-permute-start
  522.3 14.1 collective-permute-start
  536.4 14.1 collective-permute-start
  550.5 14.1 collective-permute-start
  564.6 14.1 collective-permute-start
  578.8 14.1 collective-permute-start
  592.9 14.1 collective-permute-start
  607.0 14.1 collective-permute-start
  621.1 14.1 collective-permute-start
  635.3 14.1 collective-permute-start
  649.4 14.1 collective-permute-start
  663.5 14.1 collective-permute-start
  677.6 14.1 collective-permute-start
  734.1 14.1 collective-permute-start
  833.0 14.1 collective-permute-start
  949.8 29.8 %all-to-all-start.3 = ((f32[32,4,288]{2,0,1:T(8,128)}), f32[32,4,288]{2,0,1:T(8,128)S(1)}, u32[]{:S(2)}, u32[]{:S(2)}) async-start(f32[32,4,288]{2,0,1:T(8,128)} %copy.19), calls=%async_computation.4 | async-start | bytes 393216 | tf_op jit(solution)/shard_map/all_to_all | solution.py:90
  983.7 33.3 %reduce-scatter.5.cloned.1.call-start = ((), (), s32[]{:S(2)}) async-start(), calls=%async_computation.7 | async-start | bytes 1474560 | tf_op jit(solution)/shard_map/reduce_scatter | solution.py:99
  992.5 719.2 %all-reduce.3.cloned.1.call-start = ((), (), s32[]{:S(2)}) async-start(), calls=%async_computation.8 | async-start | bytes 5308416 | tf_op jit(solution)/shard_map/psum | solution.py:110
  (101 other events, 1166.4 us)
Sparse Core Ops, SparseCore 0:
  946.9 29.6 reduce-scatter.2
  992.6 24.3 reduce-scatter.4
  1020.3 691.3 all-reduce.2
where the time goes:
time: 1720 us
  waiting for transfers between devices  1380 us (80%)
  matrix products  223 us (13%)
  starting transfers between devices  63.6 us (4%)
  blocking collectives  25.9 us (2%)
    psum x1, waiting for transfers between devices, on_device(): lax.psum((image_weight, text_weight), 'dp')  693 us
    ppermute x128, waiting for transfers between devices, shifted(): return lax.ppermute(block, axis, route)  637 us
    dot_general x64, matrix products, contribute(): jnp.dot(group_unit, text_block.T, precision=highest, preferred_element_ty...  88.2 us
    dot_general x64, matrix products, contribute(): jnp.dot(pair_grad.T, group_unit, precision=highest, preferred_element_typ...  69.8 us
    dot_general x64, matrix products, contribute(): jnp.dot(pair_grad, text_block, precision=highest, preferred_element_type=...  49.3 us
    ppermute x128, starting transfers between devices, shifted(): return lax.ppermute(block, axis, route)  49.1 us
  transfers between devices with their start and end apart: 135, of which 68 were waited for; matrix products, arithmetic and copies ran while one was open for 13% of the time, Pallas kernels for 0%

commit v1 on v0

v1 whole, which is shorter than its diff:
```python
import jax
import jax.numpy as jnp
from jax import lax
from jax.sharding import Mesh, PartitionSpec as P

logit_scale = 100.0
logit_bias = -10.0
epsilon_norm = 1e-06
GROUP = ("xl", "core")
IMAGE_AXES = ("z", "core")
TEXT_AXES = ("y", "xh", "xl")


def dot(a, b, dims):
    return lax.dot_general(
        a, b, (dims, ((), ())), precision=lax.Precision.HIGH, preferred_element_type=jnp.float32
    )


def normalize(values):
    inverse = lax.rsqrt(jnp.sum(values * values, axis=-1, keepdims=True) + epsilon_norm)
    return (values * inverse, inverse)


def on_device(image_features, text_features, image_proj, text_proj):
    rows, width = image_features.shape
    group_image = lax.all_gather(image_features, GROUP, axis=0, tiled=True)
    group_text = lax.all_gather(text_features, GROUP, axis=0, tiled=True)
    cols = jnp.stack(
        [dot(group_image, image_proj, ((1,), (0,))), dot(group_text, text_proj, ((1,), (0,)))]
    )
    raw = lax.all_to_all(cols, GROUP, split_axis=1, concat_axis=2, tiled=True)
    unit, inverse = normalize(raw)
    images = lax.all_gather(unit[0], IMAGE_AXES, axis=0, tiled=True)
    texts = lax.all_gather(unit[1], TEXT_AXES, axis=0, tiled=True)
    image_first = lax.axis_index(IMAGE_AXES) * rows
    text_first = lax.axis_index(TEXT_AXES) * rows
    shape = (images.shape[0], texts.shape[0])
    i = lax.broadcasted_iota(jnp.int32, shape, 0) - image_first
    j = lax.broadcasted_iota(jnp.int32, shape, 1) - text_first
    target = jnp.where((i == j) & (i >= 0) & (i < rows), 1.0, 0.0)
    logits = logit_scale * dot(images, texts, ((1,), (1,))) + logit_bias
    pair_grad = jax.nn.sigmoid(logits) - target
    image_sum = logit_scale * dot(pair_grad, texts, ((1,), (0,)))
    text_sum = logit_scale * dot(pair_grad, images, ((0,), (0,)))
    image_grad = lax.psum_scatter(image_sum, IMAGE_AXES, scatter_dimension=0, tiled=True)
    text_grad = lax.psum_scatter(text_sum, TEXT_AXES, scatter_dimension=0, tiled=True)
    grad = jnp.stack([image_grad, text_grad])
    dz = inverse * (grad - unit * jnp.sum(unit * grad, axis=2, keepdims=True))
    dcols = lax.all_to_all(dz, GROUP, split_axis=2, concat_axis=1, tiled=True)
    image_weight = dot(group_image, dcols[0], ((0,), (0,)))
    text_weight = dot(group_text, dcols[1], ((0,), (0,)))
    weight = jnp.concatenate([image_weight, text_weight], axis=0)
    for axis in ("z", "y", "xh"):
        weight = lax.psum_scatter(weight, axis, scatter_dimension=0, tiled=True)
    image_part = dot(dcols[0], image_proj, ((1,), (1,)))
    text_part = dot(dcols[1], text_proj, ((1,), (1,)))
    combined = lax.psum_scatter(
        jnp.concatenate([image_part, text_part], axis=1), GROUP, scatter_dimension=0, tiled=True
    )
    for axis in ("xh", "y", "z"):
        weight = lax.all_gather(weight, axis, axis=0, tiled=True)
    return (combined[:, :width], combined[:, width:], weight[:width], weight[width:])


def solution(mesh):
    fine = Mesh(mesh.devices.reshape(8, 4, 2, 2, 2), ("z", "y", "xh", "xl", "core"))
    rows = P(("z", "y", "xh", "xl", "core"), None)
    cols = P(None, GROUP)
    return jax.shard_map(
        on_device,
        mesh=fine,
        in_specs=(rows, rows, cols, cols),
        out_specs=(rows, rows, cols, cols),
        check_vma=False,
    )
```

time: 1720 us -> 544 us (0.32)
  waiting for transfers between devices: 1380 us -> 406 us
  matrix products: 223 us -> 21.6 us
  starting transfers between devices: 63.6 us -> 0.55 us
  blocking collectives: 25.9 us -> 54.1 us
  local copies, waits for them, and re-layouts: 11.3 us -> 37.6 us
    psum x1 -> x0, waiting for transfers between devices: 693 us -> none  [on_device(): lax.psum((image_weight, text_weight), 'dp')]
    ppermute x128 -> x0, waiting for transfers between devices: 637 us -> none  [shifted(): return lax.ppermute(block, axis, route)]
    dot_general x198 -> x9, matrix products: 223 us -> 21.6 us  [dot(): lax.dot_general(a, b, (dims, ((), ())), precision=lax.Precision.HIGH, pre...]
    all_gather x0 -> x3, waiting for transfers between devices: none -> 144 us  [the longest x1 52.3 us: on_device(): texts = lax.all_gather(unit[1], TEXT_AXES, axis=0, tiled=True)]
    unnamed x3 -> x12, waiting for transfers between devices: 0.05 us -> 126 us
    reduce_scatter x2 -> x3, waiting for transfers between devices: 42.2 us -> 136 us  [the longest x1 78.7 us: on_device(): lax.psum_scatter(text_sum, TEXT_AXES, scatter_dimension=0, tiled=True)]
    ppermute x128 -> x0, starting transfers between devices: 49.1 us -> none  [shifted(): return lax.ppermute(block, axis, route)]
    all_to_all x0 -> x2, blocking collectives: none -> 18.6 us  [the longest x1 9.84 us: on_device(): raw = lax.all_to_all(cols, GROUP, split_axis=1, concat_axis=2, tiled=True)]
  transfers between devices with their start and end apart: 135 -> 9, of which waited for: 68 -> 9; matrix products, arithmetic and copies ran while one was open for 13% -> 3% of each run, Pallas kernels for 0% -> 0%
where the time goes in v1:
time: 544 us; the launch traced here: 542 us
  waiting for transfers between devices  406 us (75%)
  blocking collectives  54.1 us (10%)
  local copies, waits for them, and re-layouts  37.6 us (7%)
  matrix products  21.6 us (4%)
  between operations  15.4 us (3%)
  other arithmetic  7.05 us (1%)
    unnamed x12, waiting for transfers between devices  126 us
    reduce_scatter x1, waiting for transfers between devices, on_device(): lax.psum_scatter(text_sum, TEXT_AXES, scatter_dimension=0, tiled=True)  78.7 us
    reduce_scatter x1, waiting for transfers between devices, on_device(): lax.psum_scatter(image_sum, IMAGE_AXES, scatter_dimension=0, tiled=True)  52.3 us
    all_gather x1, waiting for transfers between devices, on_device(): texts = lax.all_gather(unit[1], TEXT_AXES, axis=0, tiled=True)  52.3 us
    all_gather x1, waiting for transfers between devices, on_device(): weight = lax.all_gather(weight, axis, axis=0, tiled=True)  49.8 us
    all_gather x1, waiting for transfers between devices, on_device(): images = lax.all_gather(unit[0], IMAGE_AXES, axis=0, tiled=True)  42.1 us
    dot_general x9, matrix products, dot(): lax.dot_general(a, b, (dims, ((), ())), precision=lax.Precision.HIGH, pre...  21.6 us
    unnamed x30, local copies, waits for them, and re-layouts  20.3 us
  transfers between devices with their start and end apart: 9, of which 9 were waited for; matrix products, arithmetic and copies ran while one was open for 3% of the time, Pallas kernels for 0%

profile of v1, /device:TPU:8, one launch (start us, length us, event | category | flops | bytes accessed | tf_op | source)
XLA Modules:
  0.0 542.2 jit_solution(13400051220007235117)
XLA Ops:
  7.2 7.9 %all_gather.22 = f32[128,1152]{1,0:T(8,128)S(1)} all-gather(f32[32,1152]{1,0:T(8,128)} %param.5), channel_id=1, replica_groups=mesh['z'=8,'y'=4,'xh'=2,'xl'=2,'core'=2] {'xl','core'}, dimensions={0}, use_global_device_ids=true | all-gather | bytes 737280 | tf_op jit(solution)/shard_map/all_gather | solution.py:28
  15.1 7.8 %all_gather.21 = f32[128,1152]{1,0:T(8,128)S(1)} all-gather(f32[32,1152]{1,0:T(8,128)} %param.4), channel_id=1, replica_groups=mesh['z'=8,'y'=4,'xh'=2,'xl'=2,'core'=2] {'xl','core'}, dimensions={0}, use_global_device_ids=true | all-gather | bytes 737280 | tf_op jit(solution)/shard_map/all_gather | solution.py:27
  23.7 0.7 convolution_bitcast_fusion.3
  24.6 9.8 %all_to_all.33 = f32[2,128,288]{2,0,1:T(2,128)S(1)} all-to-all(f32[2,128,288]{2,0,1:T(2,128)S(1)} %copy.19), channel_id=1, replica_groups=mesh['z'=8,'y'=4,'xh'=2,'xl'=2,'core'=2] {'xl','core'}, dimensions={1} | all-to-all | bytes 589824 | tf_op jit(solution)/shard_map/all_to_all | solution.py:32
  34.6 1.0 copy.21
  35.6 1.2 all_to_all.27
  36.9 0.7 fusion.47
  37.7 0.7 all-gather.9.cloned.1.call-update
  38.5 52.3 %all-gather.11.cloned.1.call-done = f32[1,512,1152]{2,1,0:T(8,128)} async-done(((f32[1,32,1152]{2,1,0:T(8,128)}), f32[1,512,1152]{2,1,0:T(8,128)}) %all-gather.11.cloned.1.call-update) | async-done | bytes 2359312 | tf_op jit(solution)/shard_map/all_gather | solution.py:35
  90.8 42.1 %all-gather.9.cloned.1.call-done = f32[1,512,1152]{2,1,0:T(8,128)} async-done(((f32[1,32,1152]{2,1,0:T(8,128)}), f32[1,512,1152]{2,1,0:T(8,128)}) %all-gather.9.cloned.1.call-update) | async-done | bytes 2359312 | tf_op jit(solution)/shard_map/all_gather | solution.py:34
  132.9 5.0 fusion.35
  137.9 1.0 copy-done.5
  138.9 3.8 convolution_multiply_fusion.1
  142.8 5.7 %convolution_multiply_fusion = f32[512,1152]{1,0:T(8,128)} fusion(f32[512,512]{1,0:T(8,128)} %copy-done.5, f32[1,512,1152]{2,1,0:T(8,128)} %all-gather.9.cloned.1.call-done), kind=kOutput, calls=%fused_computation | convolution fusion | flops 1812529152 | bytes 5767168 | tf_op jit(solution)/shard_map/dot_general | solution.py:15
  148.8 52.3 %reduce-scatter.9.cloned.1.call-done = f32[32,1152]{1,0:T(8,128)} async-done(((f32[512,1152]{1,0:T(8,128)}), f32[32,1152]{1,0:T(8,128)}) %reduce-scatter.9.cloned.1.call-update) | async-done | bytes 147472 | tf_op jit(solution)/shard_map/reduce_scatter | solution.py:46
  201.2 1.8 stack.30
  202.9 0.9 copy.22
  203.9 78.7 %reduce-scatter.11.cloned.1.call-done = f32[32,1152]{1,0:T(8,128)} async-done(((f32[512,1152]{1,0:T(8,128)}), f32[32,1152]{1,0:T(8,128)}) %reduce-scatter.11.cloned.1.call-update) | async-done | bytes 147472 | tf_op jit(solution)/shard_map/reduce_scatter | solution.py:47
  282.5 1.8 stack.31
  284.3 0.9 copy.23
  285.4 1.1 fusion.41
  286.5 1.4 copy.24
  287.9 2.5 reshape.35
  290.4 8.8 %all_to_all.34 = f32[4,1,18432]{2,1,0:T(1,128)S(1)} all-to-all(f32[4,1,18432]{2,1,0:T(1,128)S(1)} %reshape.35), channel_id=1, replica_groups=mesh['z'=8,'y'=4,'xh'=2,'xl'=2,'core'=2] {'xl','core'}, dimensions={0} | all-to-all | bytes 589824 | tf_op jit(solution)/shard_map/all_to_all | solution.py:50
  299.7 1.5 reduce.2
  301.1 2.1 reshape.36
  303.2 1.5 copy.25
  304.8 1.8 convolution_bitcast_fusion
  306.6 0.7 convolution_bitcast_fusion.1
  307.4 1.7 pad_maximum_fusion
  309.1 3.6 copy.29
  314.6 47.1 %reduce-scatter.15.cloned.1.call-done = f32[288,288]{1,0:T(8,128)} async-done(((f32[2304,288]{1,0:T(8,128)}), f32[288,288]{1,0:T(8,128)}) %reduce-scatter.15.cloned.1.call-update) | async-done | bytes 331792
  361.7 2.0 copy.30
  363.7 1.5 fusion.48
  365.2 1.5 fusion.49
  366.7 43.9 %all-reduce.5.cloned.1.call-done = f32[288,288]{0,1:T(8,128)} async-done(((f32[288,288]{0,1:T(8,128)}), f32[288,288]{0,1:T(8,128)}) %all-reduce.5.cloned.1.call-update) | async-done | bytes 331792
  410.7 1.7 constant_dynamic-slice_fusion
  412.5 2.3 pad_maximum_fusion.1
  416.1 34.1 %all-reduce.7.cloned.1.call-done = f32[72,288]{0,1:T(8,128)} async-done(((f32[72,288]{0,1:T(8,128)}), f32[72,288]{0,1:T(8,128)}) %all-reduce.7.cloned.1.call-update) | async-done | bytes 82960
  450.2 1.0 dynamic-slice_bitcast_fusion
  451.3 6.4 %all-gather.2 = f32[2,36,288]{2,1,0:T(8,128)S(1)} all-gather(f32[1,36,288]{2,1,0:T(8,128)S(1)} %copy.26), channel_id=1, replica_groups=mesh['z'=8,'y'=4,'xh'=2,'xl'=2,'core'=2] {'xh'}, dimensions={0}, use_global_device_ids=true | all-gather | bytes 124416 | tf_op jit(solution)/shard_map/all_gather | solution.py:62
  457.8 13.4 %all_gather.26 = f32[288,288]{1,0:T(8,128)} all-gather(f32[72,288]{1,0:T(8,128)S(1)} %reshape.26), channel_id=1, replica_groups=mesh['z'=8,'y'=4,'xh'=2,'xl'=2,'core'=2] {'y'}, dimensions={0}, use_global_device_ids=true | all-gather | bytes 414720 | tf_op jit(solution)/shard_map/all_gather | solution.py:62
  471.2 4.9 reduce-scatter.13.cloned.1.call-done
  476.1 1.7 fusion.46
  477.8 49.8 %all-gather.7.cloned.1.call-done = f32[2304,288]{1,0:T(8,128)} async-done(((f32[288,288]{1,0:T(8,128)}), f32[2304,288]{1,0:T(8,128)}) %all-gather.7.cloned.1.call-update) | async-done | bytes 2654224 | tf_op jit(solution)/shard_map/all_gather | solution.py:62
  527.6 3.5 fusion.44
  531.1 3.0 copy.27
  534.1 1.6 copy.28
  (50 shorter events, 4.5 us)
Async XLA Ops:
  7.2 16.5 %copy-start = (f32[1152,288]{0,1:T(8,128)S(1)}, f32[1152,288]{0,1:T(8,128)}, u32[]{:S(2)}) copy-start(f32[1152,288]{0,1:T(8,128)} %param.6) | copy-start | bytes 3981316
  7.2 15.8 %copy-start.1 = (f32[1152,288]{0,1:T(8,128)S(1)}, f32[1152,288]{0,1:T(8,128)}, u32[]{:S(2)}) copy-start(f32[1152,288]{0,1:T(8,128)} %param.7) | copy-start | bytes 3981316
  7.2 83.6 %all-gather.11.cloned.1.call-start = ((), (), s32[]{:S(2)}) async-start(), calls=%async_computation.11 | async-start | bytes 2506752 | tf_op jit(solution)/shard_map/all_gather | solution.py:35
  15.1 7.9 %copy-start.4 = (f32[128,1152]{1,0:T(8,128)}, f32[128,1152]{1,0:T(8,128)S(1)}, u32[]{:S(2)}) copy-start(f32[128,1152]{1,0:T(8,128)S(1)} %all_gather.22) | copy-start | bytes 1769476
  23.0 1.4 copy-start.2
  37.7 95.2 %all-gather.9.cloned.1.call-start = ((), (), s32[]{:S(2)}) async-start(), calls=%async_computation.10 | async-start | bytes 2506752 | tf_op jit(solution)/shard_map/all_gather | solution.py:34
  38.4 162.7 %reduce-scatter.9.cloned.1.call-start = ((), (), s32[]{:S(2)}) async-start(), calls=%async_computation.6 | async-start | bytes 2506752 | tf_op jit(solution)/shard_map/reduce_scatter | solution.py:46
  132.9 6.0 %copy-start.6 = (f32[1,512,1152]{2,1,0:T(8,128)S(1)}, f32[1,512,1152]{2,1,0:T(8,128)}, u32[]{:S(2)}) copy-start(f32[1,512,1152]{2,1,0:T(8,128)} %all-gather.11.cloned.1.call-done) | copy-start | bytes 7077892
  137.9 1.0 copy-start.5
  142.8 139.8 %reduce-scatter.11.cloned.1.call-start = ((), (), s32[]{:S(2)}) async-start(), calls=%async_computation.7 | async-start | bytes 2506752 | tf_op jit(solution)/shard_map/reduce_scatter | solution.py:47
  148.6 213.1 %reduce-scatter.15.cloned.1.call-start = ((), (), s32[]{:S(2)}) async-start(), calls=%async_computation.12 | async-start | bytes 3981312
  304.7 1.9 copy-start.3
  312.7 0.7 copy-start.8
  312.7 97.9 %all-reduce.5.cloned.1.call-start = ((), (), s32[]{:S(2)}) async-start(), calls=%async_computation.13 | async-start | bytes 884736
  363.7 86.5 %all-reduce.7.cloned.1.call-start = ((), (), s32[]{:S(2)}) async-start(), calls=%async_computation.14 | async-start | bytes 294912
  412.4 2.5 copy-start.7
  412.4 63.7 %reduce-scatter.13.cloned.1.call-start = ((), (), s32[]{:S(2)}) async-start(), calls=%async_computation.8 | async-start | bytes 1474560 | tf_op jit(solution)/shard_map/reduce_scatter | solution.py:58
  414.8 112.8 %all-gather.7.cloned.1.call-start = ((), (), s32[]{:S(2)}) async-start(), calls=%async_computation.9 | async-start | bytes 3981312 | tf_op jit(solution)/shard_map/all_gather | solution.py:62
Sparse Core Ops, SparseCore 0:
  37.8 52.9 all-gather.10
  93.2 39.6 all-gather.8
  142.9 58.2 reduce-scatter.8
  204.6 77.8 reduce-scatter.10
  312.8 48.7 reduce-scatter.14
  364.6 46.0 all-reduce.4
  413.8 36.3 all-reduce.6
  453.4 22.6 reduce-scatter.12
  477.9 49.6 all-gather.6

commit v2 on v1

v2 whole, which is shorter than its diff:
```python
import jax
import jax.numpy as jnp
from jax import lax
from jax.experimental import pallas as pl
from jax.experimental.pallas import tpu as pltpu
from jax.sharding import Mesh, PartitionSpec as P

logit_scale = 100.0
logit_bias = -10.0
epsilon_norm = 1e-06
NZ, NY, NX, NC = 8, 4, 4, 2
GROUP = ("xl", "core")
MESH = pl.DeviceIdType.MESH
COPIES = 96


class Net:
    def __init__(self, send, recv):
        self.send, self.recv = send, recv
        self.z, self.y, self.c = (lax.axis_index(a) for a in ("z", "y", "core"))
        self.x = lax.axis_index("xh") * 2 + lax.axis_index("xl")
        self.started = []

    def device(self, z=None, y=None, x=None, c=None):
        z, y, x, c = (
            mine if other is None else other
            for mine, other in ((self.z, z), (self.y, y), (self.x, x), (self.c, c))
        )
        return (z, y, x // 2, x % 2, c)

    def along(self, axis, step):
        size = {"z": NZ, "y": NY, "x": NX, "c": NC}[axis]
        return self.device(**{axis: (getattr(self, axis) + step + size) % size})

    def copy(self, src, dst, device):
        k = len(self.started)
        one = pltpu.make_async_remote_copy(
            src_ref=src, dst_ref=dst, send_sem=self.send.at[k], recv_sem=self.recv.at[k],
            device_id=device, device_id_type=MESH,
        )
        one.start()
        self.started.append(one)
        return one

    def barrier(self, devices):
        semaphore = pltpu.get_barrier_semaphore()
        for device in devices:
            pl.semaphore_signal(semaphore, inc=1, device_id=device, device_id_type=MESH)
        pl.semaphore_wait(semaphore, len(devices))

    def finish(self):
        for one in self.started:
            one.wait_send()


def interleave(streams):
    streams = list(streams)
    while streams:
        left = []
        for stream in streams:
            try:
                next(stream)
                left.append(stream)
            except StopIteration:
                pass
        streams = left


def ring_gather(net, axis, n, slot, length, landed=None):
    me = getattr(net, axis)
    half = n // 2
    cut = length // 2
    parts = (pl.ds(0, cut), pl.ds(cut, length - cut))
    previous = None
    for step in range(1, half + 1):
        now = []
        for way, sign in ((0, 1), (1, -1)):
            origin = slot((me - sign * (step - 1) + n) % n)
            if previous is not None:
                previous[way].wait_recv()
            if step == half:
                origin = origin.at[parts[way]]
            now.append(net.copy(origin, origin, net.along(axis, sign)))
        if previous is not None and landed is not None:
            landed(step - 1)
            landed(1 - step)
        previous = now
        yield
    for one in previous:
        one.wait_recv()
    if landed is not None:
        landed(half)


def ring_reduce(net, axis, n, src, length, from_left, from_right, out, ready=None):
    me = getattr(net, axis)
    half = n // 2
    cut = length // 2
    parts = (pl.ds(0, cut), pl.ds(cut, length - cut))
    arrived = (from_left, from_right)
    previous = None
    for step in range(1, half + 1):
        far = half - step + 1
        now = []
        for way, sign in ((0, 1), (1, -1)):
            if ready is not None and (step > 1 or way == 0):
                ready(sign * far)
            own = src((me + sign * far + n) % n)
            if step == 1:
                piece, place = own.at[parts[way]], arrived[way].at[0, parts[way]]
            else:
                previous[way].wait_recv()
                held = arrived[way].at[step - 2]
                if step == 2:
                    held[parts[way]] = held[parts[way]] + own[parts[way]]
                    held[parts[1 - way]] = own[parts[1 - way]]
                else:
                    held[...] = held[...] + own[...]
                piece, place = held, arrived[way].at[step - 1]
            now.append(net.copy(piece, place, net.along(axis, sign)))
        previous = now
        yield
    if ready is not None:
        ready(0)
    for one in previous:
        one.wait_recv()
    out(src(me)[...] + from_left[half - 1] + from_right[half - 1])


def neighbours(net):
    return [net.along(axis, step) for axis in "zyx" for step in (1, -1)]


def gather_kernel(unit, images, texts_a, texts_b, send, recv):
    net = Net(send, recv)
    net.barrier(neighbours(net) + [net.along("c", 1)])
    images[net.c, net.z] = unit[0]
    texts_a[net.y, net.x] = unit[1, 0:2]
    texts_b[net.x, net.y] = unit[1, 2:4]
    across = []

    def image_stream(first, length):
        def slot(z):
            return images.at[net.c, z, pl.ds(first, length)]

        def landed(relative):
            block = slot((net.z + relative + NZ) % NZ)
            across.append(net.copy(block, block, net.along("c", 1)))

        landed(0)
        yield from ring_gather(net, "z", NZ, slot, length, landed)

    def text_stream(buffer, first, second, counts):
        mine = getattr(net, first)
        other = getattr(net, second)
        row = buffer.at[other]
        yield from ring_gather(net, first, counts[0], lambda i: row.at[i], 2)
        yield from ring_gather(net, second, counts[1], lambda i: buffer.at[i], counts[0])

    interleave(
        [
            image_stream(0, 2),
            text_stream(texts_a, "x", "y", (NX, NY)),
            text_stream(texts_b, "y", "x", (NY, NX)),
            image_stream(2, 2),
        ]
    )
    for one in across:
        one.wait_recv()
    net.finish()


def reduce_kernel(images, texts_a, texts_b, image_out, text_out, sibling, z0, z1, a0, a1, a2, a3, a4,
                  b0, b1, b2, b3, b4, send, recv):
    net = Net(send, recv)
    net.barrier(neighbours(net) + [net.along("c", 1)])
    pending = {}
    for relative in (4, 3, -3, 2, -2, 1, -1, 0):
        z = (net.z + relative + NZ) % NZ
        pending[relative] = net.copy(images.at[1 - net.c, z], sibling.at[z], net.along("c", 1))

    def ready(relative):
        z = (net.z + relative + NZ) % NZ
        pending[relative].wait_recv()
        sibling[z] = sibling[z] + images[net.c, z]

    def image_done(total):
        image_out[...] = total

    def text_stream(buffer, first, second, counts, scratch, place):
        middle, l1, r1, l2, r2 = scratch

        def halfway(total):
            middle[...] = total

        def done(total):
            text_out[place] = total

        yield from ring_reduce(net, first, counts[0], lambda i: buffer.at[i], counts[1], l1, r1, halfway)
        yield from ring_reduce(net, second, counts[1], lambda i: middle.at[i], 2, l2, r2, done)

    interleave(
        [
            text_stream(texts_a, "y", "x", (NY, NX), (a0, a1, a2, a3, a4), pl.ds(0, 2)),
            text_stream(texts_b, "x", "y", (NX, NY), (b0, b1, b2, b3, b4), pl.ds(2, 2)),
            ring_reduce(net, "z", NZ, lambda i: sibling.at[i], 4, z0, z1, image_done, ready),
        ]
    )
    net.finish()


A_TILES = 320
B_TILES = 328
AZ, AY = A_TILES // NZ, A_TILES // NZ // NY
BY, BZ = B_TILES // NY, 11


def weight_kernel(part, total, a_mid, b_mid, a_own, b_own, a_pair, b_pair, a_all, b_all,
                  az0, az1, ay0, ay1, by0, by1, bz0, bz1, send, recv):
    net = Net(send, recv)
    partner = net.device(x=(net.x + 2) % NX)
    net.barrier([net.along(axis, step) for axis in "zy" for step in (1, -1)] + [partner])

    def store(ref, index=...):
        def put(value):
            ref[index] = value

        return put

    def pair_sum(own, pair, put):
        one = net.copy(own, pair, partner)
        yield
        one.wait_recv()
        put(own[...] + pair[...])

    def stream_a():
        yield from ring_reduce(
            net, "z", NZ, lambda i: part.at[pl.ds(i * AZ, AZ)], AZ, az0, az1, store(a_mid)
        )
        yield from ring_reduce(
            net, "y", NY, lambda i: a_mid.at[pl.ds(i * AY, AY)], AY, ay0, ay1, store(a_own)
        )
        yield from pair_sum(a_own, a_pair, store(a_all, pl.ds(net.y * AY, AY)))
        yield from ring_gather(net, "y", NY, lambda i: a_all.at[pl.ds(i * AY, AY)], AY)
        total[pl.ds(net.z * AZ, AZ)] = a_all[...]
        yield from ring_gather(net, "z", NZ, lambda i: total.at[pl.ds(i * AZ, AZ)], AZ)

    def stream_b():
        yield from ring_reduce(
            net, "y", NY, lambda i: part.at[pl.ds(A_TILES + i * BY, BY)], BY, by0, by1,
            store(b_mid, pl.ds(0, BY)),
        )
        b_mid[pl.ds(BY, NZ * BZ - BY)] = jnp.zeros((NZ * BZ - BY, 8, 128), jnp.float32)
        yield from ring_reduce(
            net, "z", NZ, lambda i: b_mid.at[pl.ds(i * BZ, BZ)], BZ, bz0, bz1, store(b_own)
        )
        yield from pair_sum(b_own, b_pair, store(b_all, pl.ds(net.z * BZ, BZ)))
        yield from ring_gather(net, "z", NZ, lambda i: b_all.at[pl.ds(i * BZ, BZ)], BZ)
        total[pl.ds(A_TILES + net.y * BY, BY)] = b_all[pl.ds(0, BY)]
        yield from ring_gather(
            net, "y", NY, lambda i: total.at[pl.ds(A_TILES + i * BY, BY)], BY
        )

    interleave([stream_a(), stream_b()])
    net.finish()


def call(kernel, outs, scratch, collective, *args):
    vmem = pl.BlockSpec(memory_space=pltpu.VMEM)
    return pl.pallas_call(
        kernel,
        out_shape=[jax.ShapeDtypeStruct(s, jnp.float32) for s in outs],
        in_specs=[vmem] * len(args),
        out_specs=[vmem] * len(outs),
        scratch_shapes=[pltpu.VMEM(s, jnp.float32) for s in scratch]
        + [pltpu.SemaphoreType.DMA((COPIES,))] * 2,
        compiler_params=pltpu.CompilerParams(
            collective_id=collective, has_side_effects=True, vmem_limit_bytes=40 * 2**20
        ),
    )(*args)


def gather_pairs(unit):
    width = unit.shape[-1]
    tiles = unit.reshape(2, 4, 8, width)
    outs = [(NC, NZ, 4, 8, width), (NY, NX, 2, 8, width), (NX, NY, 2, 8, width)]
    images, texts_a, texts_b = call(gather_kernel, outs, [], 1, tiles)
    texts = jnp.concatenate([texts_a.reshape(-1, width), texts_b.reshape(-1, width)], axis=0)
    return (images.reshape(-1, width), texts)


def reduce_pairs(image_sum, text_sum):
    width = image_sum.shape[-1]
    tile = (8, width)
    outs = [(4,) + tile, (4,) + tile]
    scratch = [(NZ, 4) + tile, (NZ // 2, 4) + tile, (NZ // 2, 4) + tile]
    for a, b in ((NY, NX), (NX, NY)):
        scratch += [(b, 2) + tile] + [(a // 2, b, 2) + tile] * 2 + [(b // 2, 2) + tile] * 2
    count = text_sum.shape[0] // 2
    image, text = call(
        reduce_kernel, outs, scratch, 2,
        image_sum.reshape((NC, NZ, 4) + tile),
        text_sum[:count].reshape((NY, NX, 2) + tile),
        text_sum[count:].reshape((NX, NY, 2) + tile),
    )
    return (image.reshape(32, width), text.reshape(32, width))


def reduce_weights(part):
    high, wide = part.shape
    tiles = part.reshape(high // 8, 8, wide // 128, 128).transpose(0, 2, 1, 3).reshape(-1, 8, 128)
    lengths = [AZ, NZ * BZ, AY, BZ, AY, BZ, AZ, NZ * BZ]
    scratch = [(n, 8, 128) for n in lengths]
    scratch += [(NZ // 2, AZ, 8, 128)] * 2 + [(NY // 2, AY, 8, 128)] * 2
    scratch += [(NY // 2, BY, 8, 128)] * 2 + [(NZ // 2, BZ, 8, 128)] * 2
    (total,) = call(weight_kernel, [tiles.shape], scratch, 3, tiles)
    return total.reshape(high // 8, wide // 128, 8, 128).transpose(0, 2, 1, 3).reshape(high, wide)


def dot(a, b, dims):
    return lax.dot_general(
        a, b, (dims, ((), ())), precision=lax.Precision.HIGH, preferred_element_type=jnp.float32
    )


def normalize(values):
    inverse = lax.rsqrt(jnp.sum(values * values, axis=-1, keepdims=True) + epsilon_norm)
    return (values * inverse, inverse)


def pair_target(rows):
    z, y, c = (lax.axis_index(a) for a in ("z", "y", "core"))
    x = lax.axis_index("xh") * 2 + lax.axis_index("xl")
    i = lax.broadcasted_iota(jnp.int32, (16 * rows, 16 * rows), 0) - (c * NZ + z) * rows
    j = lax.broadcasted_iota(jnp.int32, (16 * rows, 16 * rows), 1)
    half, count = rows // 2, 8 * rows
    a = j - (y * NX + x) * half
    b = j - count - (x * NY + y) * half + half
    same_a = (i == a) & (a >= 0) & (a < half)
    same_b = (i == b) & (b >= half) & (b < rows)
    return jnp.where(same_a | same_b, 1.0, 0.0)


def on_device(image_features, text_features, image_proj, text_proj):
    rows, width = image_features.shape
    group_image = lax.all_gather(image_features, GROUP, axis=0, tiled=True)
    group_text = lax.all_gather(text_features, GROUP, axis=0, tiled=True)
    cols = jnp.stack(
        [dot(group_image, image_proj, ((1,), (0,))), dot(group_text, text_proj, ((1,), (0,)))]
    )
    raw = lax.all_to_all(cols, GROUP, split_axis=1, concat_axis=2, tiled=True)
    unit, inverse = normalize(raw)
    images, texts = gather_pairs(unit)
    logits = logit_scale * dot(images, texts, ((1,), (1,))) + logit_bias
    pair_grad = jax.nn.sigmoid(logits) - pair_target(rows)
    image_sum = logit_scale * dot(pair_grad, texts, ((1,), (0,)))
    text_sum = logit_scale * dot(pair_grad, images, ((0,), (0,)))
    grad = jnp.stack(reduce_pairs(image_sum, text_sum))
    dz = inverse * (grad - unit * jnp.sum(unit * grad, axis=2, keepdims=True))
    dcols = lax.all_to_all(dz, GROUP, split_axis=2, concat_axis=1, tiled=True)
    image_weight = dot(dcols[0], group_image, ((0,), (0,)))
    text_weight = dot(dcols[1], group_text, ((0,), (0,)))
    weight = reduce_weights(jnp.concatenate([image_weight, text_weight], axis=0))
    image_part = dot(dcols[0], image_proj, ((1,), (1,)))
    text_part = dot(dcols[1], text_proj, ((1,), (1,)))
    combined = lax.psum_scatter(
        jnp.concatenate([image_part, text_part], axis=1), GROUP, scatter_dimension=0, tiled=True
    )
    columns = image_proj.shape[1]
    return (combined[:, :width], combined[:, width:], weight[:columns].T, weight[columns:].T)


def solution(mesh):
    fine = Mesh(mesh.devices.reshape(NZ, NY, 2, 2, NC), ("z", "y", "xh", "xl", "core"))
    rows = P(("z", "y", "xh", "xl", "core"), None)
    cols = P(None, GROUP)
    return jax.shard_map(
        on_device,
        mesh=fine,
        in_specs=(rows, rows, cols, cols),
        out_specs=(rows, rows, cols, cols),
        check_vma=False,
    )
```

time: 544 us -> 208 us (0.38)
  waiting for transfers between devices: 406 us -> 7.11 us
  Pallas kernels: 0 us -> 121 us
  blocking collectives: 54.1 us -> 24.5 us
  local copies, waits for them, and re-layouts: 37.6 us -> 19.8 us
  matrix products: 21.6 us -> 11.6 us
    all_gather x3 -> x0, waiting for transfers between devices: 144 us -> none  [the longest x1 52.3 us: on_device(): texts = lax.all_gather(unit[1], TEXT_AXES, axis=0, tiled=True)]
    reduce_scatter x2 -> x0, waiting for transfers between devices: 131 us -> none  [the longest x1 78.7 us: on_device(): lax.psum_scatter(text_sum, TEXT_AXES, scatter_dimension=0, tiled=True)]
    unnamed x12 -> x1, waiting for transfers between devices: 126 us -> 0.02 us
    pallas_call x0 -> x3, Pallas kernels: none -> 121 us  [call(): pl.pallas_call(kernel, out_shape=[jax.ShapeDtypeStruct(s, jnp.float32) fo...]
    all_gather x2 -> x0, blocking collectives: 19.8 us -> none  [on_device(): weight = lax.all_gather(weight, axis, axis=0, tiled=True)]
    unnamed x30 -> x16, local copies, waits for them, and re-layouts: 20.3 us -> 4.98 us
    dot_general x9, matrix products: 21.6 us -> 11.6 us  [dot(): lax.dot_general(a, b, (dims, ((), ())), precision=lax.Precision.HIGH, pre...]
    all_to_all x1 -> x0, blocking collectives: 9.84 us -> none  [on_device(): raw = lax.all_to_all(cols, GROUP, split_axis=1, concat_axis=2, tiled=True)]
  transfers between devices with their start and end apart: 9 -> 2, of which waited for: 9 -> 1; matrix products, arithmetic and copies ran while one was open for 3% -> 2% of each run, Pallas kernels for 0% -> 31%
where the time goes in v2:
time: 208 us; the launch traced here: 206 us
  Pallas kernels  121 us (58%)
  blocking collectives  24.5 us (12%)
  local copies, waits for them, and re-layouts  19.8 us (10%)
  between operations  14.3 us (7%)
  matrix products  11.6 us (6%)
  waiting for transfers between devices  7.11 us (3%)
  other arithmetic  4.31 us (2%)
  starting transfers between devices  3.68 us (2%)
    pallas_call x3, Pallas kernels, call(): pl.pallas_call(kernel, out_shape=[jax.ShapeDtypeStruct(s, jnp.float32) fo...  121 us
    dot_general x9, matrix products, dot(): lax.dot_general(a, b, (dims, ((), ())), precision=lax.Precision.HIGH, pre...  11.6 us
    all_to_all x1, blocking collectives, on_device(): dcols = lax.all_to_all(dz, GROUP, split_axis=2, concat_axis=1, tiled=True)  8.75 us
    all_gather x1, blocking collectives, on_device(): group_image = lax.all_gather(image_features, GROUP, axis=0, tiled=True)  7.87 us
    all_gather x1, blocking collectives, on_device(): group_text = lax.all_gather(text_features, GROUP, axis=0, tiled=True)  7.85 us
    all_to_all x1, waiting for transfers between devices, on_device(): raw = lax.all_to_all(cols, GROUP, split_axis=1, concat_axis=2, tiled=True)  7.1 us
    unnamed x16, local copies, waits for them, and re-layouts  4.98 us
  transfers between devices with their start and end apart: 2, of which 1 were waited for; matrix products, arithmetic and copies ran while one was open for 2% of the time, Pallas kernels for 31%

profile of v2, /device:TPU:8, one launch (start us, length us, event | category | flops | bytes accessed | tf_op | source)
XLA Modules:
  0.0 206.2 jit_solution(5411671202297897776)
XLA Ops:
  7.2 0.0 copy-start
  7.2 0.0 copy-start.1
  7.2 7.9 %all_gather.6 = f32[128,1152]{1,0:T(8,128)S(1)} all-gather(f32[32,1152]{1,0:T(8,128)} %param.4), channel_id=1, replica_groups=mesh['z'=8,'y'=4,'xh'=2,'xl'=2,'core'=2] {'xl','core'}, dimensions={0}, use_global_device_ids=true | all-gather | bytes 737280 | tf_op jit(solution)/shard_map/all_gather | solution.py:346
  15.1 7.8 %all_gather.7 = f32[128,1152]{1,0:T(8,128)S(1)} all-gather(f32[32,1152]{1,0:T(8,128)} %param.5), channel_id=1, replica_groups=mesh['z'=8,'y'=4,'xh'=2,'xl'=2,'core'=2] {'xl','core'}, dimensions={0}, use_global_device_ids=true | all-gather | bytes 737280 | tf_op jit(solution)/shard_map/all_gather | solution.py:347
  22.9 0.7 convolution_bitcast_fusion.1
  23.6 0.7 convolution_bitcast_fusion
  24.4 0.9 copy.20
  25.3 3.5 %all-to-all-start = ((f32[2,128,288]{2,0,1:T(2,128)}), f32[2,128,288]{2,0,1:T(2,128)S(1)}, u32[]{:S(2)}, u32[]{:S(2)}) async-start(f32[2,128,288]{2,0,1:T(2,128)} %copy.20), calls=%async_computation | async-start | bytes 786432 | tf_op jit(solution)/shard_map/all_to_all | solution.py:351
  28.7 0.2 reduce-scatter.2.cloned.1.call-start
  29.1 7.1 %all-to-all-done = f32[2,128,288]{2,0,1:T(2,128)S(1)} async-done(((f32[2,128,288]{2,0,1:T(2,128)}), f32[2,128,288]{2,0,1:T(2,128)S(1)}, u32[]{:S(2)}, u32[]{:S(2)}) %all-to-all-start) | async-done | bytes 294944 | tf_op jit(solution)/shard_map/all_to_all | solution.py:351
  36.2 0.1 multiply_reduce_fusion
  36.3 0.3 copy.22
  36.6 0.9 all_to_all.30
  37.5 0.9 all_to_all.29
  38.4 0.1 rsqrt.13
  38.5 1.1 broadcast_multiply_fusion.unit
  39.6 29.5 %shard_map.75 = (f32[2,8,4,8,1152]{4,3,2,1,0:T(8,128)S(1)}, f32[4,4,2,8,1152]{4,3,2,1,0:T(8,128)S(1)}, f32[4,4,2,8,1152]{4,3,2,1,0:T(8,128)S(1)}) custom-call(f32[2,4,8,1152]{3,2,1,0:T(8,128)S(1)} %broadcast_multiply_fusion.unit), custom_call_target="tpu_custom_call" | custom-call | tf_op jit(solution)/shard_map/pallas_call | solution.py:270
  69.1 2.7 %fusion.7 = f32[512,512]{1,0:T(8,128)S(1)} fusion(f32[512,1152]{1,0:T(8,128)S(1)} %bitcast.58, f32[256,1152]{1,0:T(8,128)S(1)} %bitcast.62, f32[256,1152]{1,0:T(8,128)S(1)} %bitcast.60, s32[512]{0:T(512)S(1)} %get-tuple-element.26, s32[512]{0:T(512)S(1)} %get-tuple-element.27, s32[512]{0:T(512)S(1)} %iota_subtract_fusion.1, ...), kind=kOutput, calls=%fused_computation.16 | convolution fusion | flops 1816199168 | bytes 5775360 | tf_op jit(solution)/shard_map/dot_general | solution.py:321
  71.8 2.3 %convolution_multiply_fusion = f32[512,1152]{1,0:T(8,128)S(1)} fusion(f32[512,512]{1,0:T(8,128)S(1)} %fusion.7, f32[512,1152]{1,0:T(8,128)S(1)} %bitcast.59), kind=kOutput, calls=%fused_computation | convolution fusion | flops 1812529152 | bytes 5767168 | tf_op jit(solution)/shard_map/dot_general | solution.py:321
  74.2 2.3 %convolution_multiply_fusion.1 = f32[512,1152]{1,0:T(8,128)S(1)} fusion(f32[512,512]{1,0:T(8,128)S(1)} %fusion.7, f32[256,1152]{1,0:T(8,128)S(1)} %bitcast.63, f32[256,1152]{1,0:T(8,128)S(1)} %bitcast.61), kind=kOutput, calls=%fused_computation.1 | convolution fusion | flops 1813118976 | bytes 5767168 | tf_op jit(solution)/shard_map/dot_general | solution.py:321
  76.5 0.2 fusion.14
  76.7 27.0 %shard_map.76 = (f32[4,8,1152]{2,1,0:T(8,128)S(1)}, f32[4,8,1152]{2,1,0:T(8,128)S(1)}) custom-call(f32[2,8,4,8,1152]{4,3,2,1,0:T(8,128)S(1)} %bitcast.55, f32[4,4,2,8,1152]{4,3,2,1,0:T(8,128)S(1)} %bitcast.57, f32[4,4,2,8,1152]{4,3,2,1,0:T(8,128)S(1)} %bitcast.56), custom_call_target="tpu_custom_call" | custom-call | tf_op jit(solution)/shard_map/pallas_call | solution.py:270
  103.7 0.8 stack.22
  104.6 0.9 copy.24
  105.5 0.8 stack.23
  106.3 1.0 copy.25
  107.3 0.2 fusion.8
  107.5 0.1 fusion.9
  107.7 1.6 copy.26
  109.3 2.5 %reshape.70 = f32[4,1,18432]{2,1,0:T(1,128)S(1)} reshape(f32[1152,2,32]{2,1,0:T(2,128)} %bitcast.69) | data formatting | bytes 589824
  111.8 8.8 %all_to_all.36 = f32[4,1,18432]{2,1,0:T(1,128)S(1)} all-to-all(f32[4,1,18432]{2,1,0:T(1,128)S(1)} %reshape.70), channel_id=1, replica_groups=mesh['z'=8,'y'=4,'xh'=2,'xl'=2,'core'=2] {'xl','core'}, dimensions={0} | all-to-all | bytes 589824 | tf_op jit(solution)/shard_map/all_to_all | solution.py:360
  120.5 0.5 broadcast.60
  121.0 1.5 reduce.2
  122.5 2.1 reshape.71
  124.5 2.4 %copy.30 = f32[2,32,4,288]{3,2,1,0:T(4,128)S(1)} copy(f32[2,32,4,288]{1,0,3,2:T(2,128)} %bitcast.70) | data formatting | bytes 589824 | tf_op jit(solution)/shard_map/all_to_all | solution.py:360
  127.0 0.7 fusion.18
  127.7 0.7 fusion.17
  128.4 0.0 copy-start.5
  128.4 1.1 pad_maximum_fusion.14
  129.5 0.0 reduce-scatter.2.cloned.1.call-update
  129.5 0.1 copy-done.5
  129.6 0.7 fusion.20
  130.4 0.3 copy-done.3
  130.7 0.7 fusion.19
  131.4 0.2 pad_maximum_fusion
  131.6 64.4 %shard_map.77 = f32[648,8,128]{2,1,0:T(8,128)S(1)} custom-call(f32[648,8,128]{2,1,0:T(8,128)S(1)} %bitcast.54), custom_call_target="tpu_custom_call" | custom-call | tf_op jit(solution)/shard_map/pallas_call | solution.py:270
  196.0 1.7 slice_bitcast_fusion
  197.7 1.7 fusion.16
  (20 shorter events, 0.2 us)
Async XLA Ops:
  7.2 16.5 %copy-start = (f32[1152,288]{0,1:T(8,128)S(1)}, f32[1152,288]{0,1:T(8,128)}, u32[]{:S(2)}) copy-start(f32[1152,288]{0,1:T(8,128)} %param.7) | copy-start | bytes 3981316
  7.2 15.7 %copy-start.1 = (f32[1152,288]{0,1:T(8,128)S(1)}, f32[1152,288]{0,1:T(8,128)}, u32[]{:S(2)}) copy-start(f32[1152,288]{0,1:T(8,128)} %param.6) | copy-start | bytes 3981316
  15.1 8.5 %copy-start.2 = (f32[128,1152]{1,0:T(8,128)}, f32[128,1152]{1,0:T(8,128)S(1)}, u32[]{:S(2)}) copy-start(f32[128,1152]{1,0:T(8,128)S(1)} %all_gather.6) | copy-start | bytes 1769476
  22.9 1.4 copy-start.4
  25.3 10.9 %all-to-all-start = ((f32[2,128,288]{2,0,1:T(2,128)}), f32[2,128,288]{2,0,1:T(2,128)S(1)}, u32[]{:S(2)}, u32[]{:S(2)}) async-start(f32[2,128,288]{2,0,1:T(2,128)} %copy.20), calls=%async_computation | async-start | bytes 786432 | tf_op jit(solution)/shard_map/all_to_all | solution.py:351
  28.7 168.9 %reduce-scatter.2.cloned.1.call-start = ((), (), s32[]{:S(2)}) async-start(), calls=%async_computation.3 | async-start | bytes 1474560 | tf_op jit(solution)/shard_map/reduce_scatter | solution.py:366
  106.3 1.2 copy-start.6
  128.4 1.3 copy-start.5
  129.6 1.1 copy-start.3
Sparse Core Ops, SparseCore 0:
  129.6 23.0 reduce-scatter.1

commit v3 on v2

v3 whole, which is shorter than its diff:
```python
import jax
import jax.numpy as jnp
from jax import lax
from jax.experimental import pallas as pl
from jax.experimental.pallas import tpu as pltpu
from jax.sharding import Mesh, PartitionSpec as P

logit_scale = 100.0
logit_bias = -10.0
epsilon_norm = 1e-06
NZ, NY, NX, NC = 8, 4, 4, 2
GROUP = ("xl", "core")
MESH = pl.DeviceIdType.MESH
COPIES = 176


class Net:
    def __init__(self, send, recv):
        self.send, self.recv = send, recv
        self.z, self.y, self.c = (lax.axis_index(a) for a in ("z", "y", "core"))
        self.x = lax.axis_index("xh") * 2 + lax.axis_index("xl")
        self.started = []

    def device(self, z=None, y=None, x=None, c=None):
        z, y, x, c = (
            mine if other is None else other
            for mine, other in ((self.z, z), (self.y, y), (self.x, x), (self.c, c))
        )
        return (z, y, x // 2, x % 2, c)

    def along(self, axis, step):
        size = {"z": NZ, "y": NY, "x": NX, "c": NC}[axis]
        return self.device(**{axis: (getattr(self, axis) + step + size) % size})

    def copy(self, src, dst, device):
        k = len(self.started)
        one = pltpu.make_async_remote_copy(
            src_ref=src, dst_ref=dst, send_sem=self.send.at[k], recv_sem=self.recv.at[k],
            device_id=device, device_id_type=MESH,
        )
        one.start()
        self.started.append(one)
        return one

    def barrier(self, devices):
        semaphore = pltpu.get_barrier_semaphore()
        for device in devices:
            pl.semaphore_signal(semaphore, inc=1, device_id=device, device_id_type=MESH)
        pl.semaphore_wait(semaphore, len(devices))

    def finish(self):
        for one in self.started:
            one.wait_send()


def interleave(streams):
    streams = list(streams)
    while streams:
        left = []
        for stream in streams:
            try:
                next(stream)
                left.append(stream)
            except StopIteration:
                pass
        streams = left


def ring_gather(net, axis, n, slot, length, landed=None):
    me = getattr(net, axis)
    half = n // 2
    cut = length // 2
    parts = (pl.ds(0, cut), pl.ds(cut, length - cut))
    previous = None
    for step in range(1, half + 1):
        now = []
        for way, sign in ((0, 1), (1, -1)):
            origin = slot((me - sign * (step - 1) + n) % n)
            if previous is not None:
                previous[way].wait_recv()
            if step == half:
                origin = origin.at[parts[way]]
            now.append(net.copy(origin, origin, net.along(axis, sign)))
        if previous is not None and landed is not None:
            landed(step - 1)
            landed(1 - step)
        previous = now
        yield
    for one in previous:
        one.wait_recv()
    if landed is not None:
        landed(half)


def ring_reduce(net, axis, n, src, length, from_left, from_right, out, ready=None):
    me = getattr(net, axis)
    half = n // 2
    cut = length // 2
    parts = (pl.ds(0, cut), pl.ds(cut, length - cut))
    arrived = (from_left, from_right)
    previous = None
    for step in range(1, half + 1):
        far = half - step + 1
        now = []
        for way, sign in ((0, 1), (1, -1)):
            if ready is not None and (step > 1 or way == 0):
                ready(sign * far)
            own = src((me + sign * far + n) % n)
            if step == 1:
                piece, place = own.at[parts[way]], arrived[way].at[0, parts[way]]
            else:
                previous[way].wait_recv()
                held = arrived[way].at[step - 2]
                if step == 2:
                    held[parts[way]] = held[parts[way]] + own[parts[way]]
                    held[parts[1 - way]] = own[parts[1 - way]]
                else:
                    held[...] = held[...] + own[...]
                piece, place = held, arrived[way].at[step - 1]
            now.append(net.copy(piece, place, net.along(axis, sign)))
        previous = now
        yield
    if ready is not None:
        ready(0)
    for one in previous:
        one.wait_recv()
    out(src(me)[...] + from_left[half - 1] + from_right[half - 1])


def neighbours(net):
    return [net.along(axis, step) for axis in "zyx" for step in (1, -1)]


def group_places(net):
    low, high = net.x % 2, net.x - net.x % 2
    here = (low * 2 + net.c, low * 2 + 1 - net.c)
    there = ((1 - low) * 2 + net.c, (1 - low) * 2 + 1 - net.c)
    other = high + 1 - low
    devices = (net.device(c=1 - net.c), net.device(x=other), net.device(x=other, c=1 - net.c))
    return here + there, devices


def greet(net):
    _, (_, _, diagonal) = group_places(net)
    net.barrier(neighbours(net) + [net.along("c", 1), diagonal])


def halves(value):
    high = value.astype(jnp.bfloat16)
    return (high, (value - high.astype(jnp.float32)).astype(jnp.bfloat16))


def dot3(a, b, dims):
    def one(p, q):
        return lax.dot_general(p, q, (dims, ((), ())), preferred_element_type=jnp.float32)

    return one(a[0], b[0]) + (one(a[0], b[1]) + one(a[1], b[0]))


def front_kernel(image_x, text_x, image_w, text_w, images, texts, group, unit, inverse,
                 col_out, col_in, send, recv):
    net = Net(send, recv)
    (me, sib, far, diag), (to_sib, to_far, to_diag) = group_places(net)
    rows, width = image_x.shape
    part = image_w.shape[1]
    greet(net)
    group[0, me] = image_x[...]
    group[1, me] = text_x[...]
    first = []
    for t in range(2):
        block = group.at[t, me]
        first.append((net.copy(block, block, to_far), net.copy(block, block, to_sib)))
    across = []

    def prepare(t, w):
        weights = halves(w[...])
        first[t][0].wait_recv()
        block = group.at[t, far]
        onward = net.copy(block, block, to_sib)
        yield
        first[t][1].wait_recv()
        onward.wait_recv()
        cols = dot3(halves(group[t].reshape(4 * rows, width)), weights, ((1,), (0,)))
        col_out[t] = cols.reshape(4, rows, part)
        copies = [
            net.copy(col_out.at[t, place], col_in.at[t, me], device)
            for place, device in ((far, to_far), (diag, to_diag), (sib, to_sib))
        ]
        col_in[t, me] = col_out[t, me]
        yield
        for one in copies:
            one.wait_recv()
        raw = jnp.concatenate([col_in[t, k] for k in range(4)], axis=1)
        scale = lax.rsqrt(jnp.sum(raw * raw, axis=1, keepdims=True) + epsilon_norm)
        unit[t] = raw * scale
        inverse[t] = jnp.broadcast_to(scale, (rows, 128))

    def image_start():
        yield from prepare(0, image_w)
        images[net.c, net.z] = unit[0].reshape(4, 8, width)

    def text_start():
        yield from prepare(1, text_w)
        tiles = unit[1].reshape(4, 8, width)
        texts[0, net.y, net.x] = tiles[0:2]
        texts[1, net.x, net.y] = tiles[2:4]

    def image_stream(first, length):
        def slot(z):
            return images.at[net.c, z, pl.ds(first, length)]

        def landed(relative):
            block = slot((net.z + relative + NZ) % NZ)
            across.append(net.copy(block, block, net.along("c", 1)))

        yield from ring_gather(net, "z", NZ, slot, length, landed)

    def text_stream(half, first, second, counts):
        buffer = texts.at[half]
        row = buffer.at[getattr(net, second)]
        yield from ring_gather(net, first, counts[0], lambda i: row.at[i], 2)
        yield from ring_gather(net, second, counts[1], lambda i: buffer.at[i], counts[0])

    interleave([image_start(), text_start()])
    own = images.at[net.c, net.z]
    streams = [
        image_stream(0, 2),
        text_stream(0, "x", "y", (NX, NY)),
        text_stream(1, "y", "x", (NY, NX)),
        image_stream(2, 2),
    ]
    for stream in streams:
        next(stream)
    across.append(net.copy(own, own, net.along("c", 1)))
    interleave(streams)
    for one in across:
        one.wait_recv()
    net.finish()


A_STREAMS, B_STREAMS = 2, 2
AZ, AY = 20, 5
BY, BZ = 41, 6
A_TILES = A_STREAMS * NZ * AZ


def weight_stream_a(net, partner, base, part, total, mid, own, pair, every, z0, z1, y0, y1):
    def put(ref, index=...):
        def store(value):
            ref[index] = value

        return store

    yield from ring_reduce(
        net, "z", NZ, lambda i: part.at[pl.ds(base + i * AZ, AZ)], AZ, z0, z1, put(mid)
    )
    yield from ring_reduce(net, "y", NY, lambda i: mid.at[pl.ds(i * AY, AY)], AY, y0, y1, put(own))
    one = net.copy(own, pair, partner)
    yield
    one.wait_recv()
    every[pl.ds(net.y * AY, AY)] = own[...] + pair[...]
    yield from ring_gather(net, "y", NY, lambda i: every.at[pl.ds(i * AY, AY)], AY)
    total[pl.ds(base + net.z * AZ, AZ)] = every[...]
    yield from ring_gather(net, "z", NZ, lambda i: total.at[pl.ds(base + i * AZ, AZ)], AZ)


def weight_stream_b(net, partner, base, part, total, mid, own, pair, every, y0, y1, z0, z1):
    def put(ref, index=...):
        def store(value):
            ref[index] = value

        return store

    mid[pl.ds(BY, NZ * BZ - BY)] = jnp.zeros((NZ * BZ - BY, 8, 128), jnp.float32)
    yield from ring_reduce(
        net, "y", NY, lambda i: part.at[pl.ds(base + i * BY, BY)], BY, y0, y1, put(mid, pl.ds(0, BY))
    )
    yield from ring_reduce(net, "z", NZ, lambda i: mid.at[pl.ds(i * BZ, BZ)], BZ, z0, z1, put(own))
    one = net.copy(own, pair, partner)
    yield
    one.wait_recv()
    every[pl.ds(net.z * BZ, BZ)] = own[...] + pair[...]
    yield from ring_gather(net, "z", NZ, lambda i: every.at[pl.ds(i * BZ, BZ)], BZ)
    total[pl.ds(base + net.y * BY, BY)] = every[pl.ds(0, BY)]
    yield from ring_gather(net, "y", NY, lambda i: total.at[pl.ds(base + i * BY, BY)], BY)


def back_shapes(width, part):
    tile, small = (8, width), (8, 128)
    rows = 32
    shapes = [(NZ, 4) + tile]
    shapes += [(NZ // 2, 2) + tile] * 4
    for a, b in ((NY, NX), (NX, NY)):
        shapes += [(b, 2) + tile] + [(a // 2, b, 2) + tile] * 2 + [(b // 2, 2) + tile] * 2
    shapes += [(2, 4) + tile]
    shapes += [(2, 4, rows, part)] * 2
    shapes += [(2 * part // 8 * (width // 128),) + small]
    shapes += [(2, 4, rows, width), (2, 2, rows, width), (2, rows, width)]
    for _ in range(A_STREAMS):
        shapes += [(n,) + small for n in (AZ, AY, AY, AZ)]
        shapes += [(NZ // 2, AZ) + small] * 2 + [(NY // 2, AY) + small] * 2
    for _ in range(B_STREAMS):
        shapes += [(n,) + small for n in (NZ * BZ, BZ, BZ, NZ * BZ)]
        shapes += [(NY // 2, BY) + small] * 2 + [(NZ // 2, BZ) + small] * 2
    return shapes


def back_kernel(images, texts, unit, inverse, group, image_w, text_w, image_out, text_out, total,
                sibling, *rest):
    send, recv = rest[-2:]
    rest = list(rest[:-2])

    def take(count):
        taken = rest[:count]
        del rest[:count]
        return taken

    z_low, z_high = take(2), take(2)
    text_scratch = (take(5), take(5))
    grad, d_out, d_in, part, feature, feature_in, feature_sum = take(7)
    a_scratch = [take(8) for _ in range(A_STREAMS)]
    b_scratch = [take(8) for _ in range(B_STREAMS)]
    net = Net(send, recv)
    (me, sib, far, diag), (to_sib, to_far, to_diag) = group_places(net)
    partner = net.device(x=(net.x + 2) % NX)
    rows, width = image_out.shape
    columns = image_w.shape[1]
    semaphores = [net.device(x=(net.x + 2) % NX)]
    _, (_, _, diagonal) = group_places(net)
    net.barrier(neighbours(net) + [net.along("c", 1), diagonal] + semaphores)
    pending = {}
    order = (4, 3, -3, 2, -2, 1, -1, 0)
    for relative in order:
        z = (net.z + relative + NZ) % NZ
        pending[relative] = net.copy(images.at[1 - net.c, z], sibling.at[z], net.along("c", 1))
    summed = set()

    def ready(relative):
        if relative in summed:
            return
        summed.add(relative)
        z = (net.z + relative + NZ) % NZ
        pending[relative].wait_recv()
        sibling[z] = sibling[z] + images[net.c, z]

    def put(ref, *index):
        def store(value):
            ref[index] = value

        return store

    def image_stream(first, scratch):
        yield from ring_reduce(
            net, "z", NZ, lambda i: sibling.at[i, pl.ds(first, 2)], 2, *scratch,
            put(grad, 0, pl.ds(first, 2)), ready,
        )

    def text_stream(half, first, second, counts, scratch):
        buffer = texts.at[half]
        middle, l1, r1, l2, r2 = scratch
        yield from ring_reduce(
            net, first, counts[0], lambda i: buffer.at[i], counts[1], l1, r1, put(middle, ...)
        )
        yield from ring_reduce(
            net, second, counts[1], lambda i: middle.at[i], 2, l2, r2,
            put(grad, 1, pl.ds(half * 2, 2)),
        )

    interleave(
        [
            image_stream(0, z_low),
            text_stream(0, "y", "x", (NY, NX), text_scratch[0]),
            text_stream(1, "x", "y", (NX, NY), text_scratch[1]),
            image_stream(2, z_high),
        ]
    )

    exchanged = []
    for t in range(2):
        g, u = grad[t].reshape(rows, width), unit[t]
        dz = inverse[t][:, :1] * (g - u * jnp.sum(u * g, axis=1, keepdims=True))
        for k in range(4):
            d_out[t, k] = dz[:, k * columns : (k + 1) * columns]
        exchanged.append(
            [
                net.copy(d_out.at[t, place], d_in.at[t, me], device)
                for place, device in ((far, to_far), (diag, to_diag), (sib, to_sib))
            ]
        )
        d_in[t, me] = d_out[t, me]

    per_tower = columns // 8
    lanes = width // 128
    feature_first = []
    for t, w in ((0, image_w), (1, text_w)):
        for one in exchanged[t]:
            one.wait_recv()
        dcols = halves(d_in[t].reshape(4 * rows, columns))
        x = halves(group[t].reshape(4 * rows, width))
        weight = dot3(dcols, x, ((0,), (0,)))
        for j in range(lanes):
            part[pl.ds((t * lanes + j) * per_tower, per_tower)] = weight[
                :, j * 128 : (j + 1) * 128
            ].reshape(per_tower, 8, 128)

    def feature_stream():
        for t, w in ((0, image_w), (1, text_w)):
            dcols = halves(d_in[t].reshape(4 * rows, columns))
            terms = dot3(dcols, halves(w[...]), ((1,), (1,)))
            feature[t] = terms.reshape(4, rows, width)
            feature_first.append(
                (
                    net.copy(feature.at[t, diag], feature_in.at[t, 0], to_sib),
                    net.copy(feature.at[t, sib], feature_in.at[t, 1], to_sib),
                )
            )
        yield
        last = []
        for t in range(2):
            feature_first[t][0].wait_recv()
            feature_in[t, 0] = feature_in[t, 0] + feature[t, far]
            last.append(net.copy(feature_in.at[t, 0], feature_sum.at[t], to_far))
        for _ in range(6):
            yield
        for t, out in ((0, image_out), (1, text_out)):
            feature_first[t][1].wait_recv()
            last[t].wait_recv()
            out[...] = feature[t, me] + feature_in[t, 1] + feature_sum[t]

    streams = []
    for k in range(max(A_STREAMS, B_STREAMS)):
        if k < A_STREAMS:
            streams.append(
                weight_stream_a(net, partner, k * NZ * AZ, part, total, *a_scratch[k])
            )
        if k < B_STREAMS:
            streams.append(
                weight_stream_b(net, partner, A_TILES + k * NY * BY, part, total, *b_scratch[k])
            )
    interleave(streams + [feature_stream()])
    net.finish()


def call(kernel, outs, scratch, collective, *args):
    vmem = pl.BlockSpec(memory_space=pltpu.VMEM)
    return pl.pallas_call(
        kernel,
        out_shape=[jax.ShapeDtypeStruct(s, jnp.float32) for s in outs],
        in_specs=[vmem] * len(args),
        out_specs=[vmem] * len(outs),
        scratch_shapes=[pltpu.VMEM(s, jnp.float32) for s in scratch]
        + [pltpu.SemaphoreType.DMA((COPIES,))] * 2,
        compiler_params=pltpu.CompilerParams(
            collective_id=collective, has_side_effects=True, vmem_limit_bytes=52 * 2**20
        ),
    )(*args)


def dot(a, b, dims):
    return lax.dot_general(
        a, b, (dims, ((), ())), precision=lax.Precision.HIGH, preferred_element_type=jnp.float32
    )


def pair_target(rows):
    z, y, c = (lax.axis_index(a) for a in ("z", "y", "core"))
    x = lax.axis_index("xh") * 2 + lax.axis_index("xl")
    i = lax.broadcasted_iota(jnp.int32, (16 * rows, 16 * rows), 0) - (c * NZ + z) * rows
    j = lax.broadcasted_iota(jnp.int32, (16 * rows, 16 * rows), 1)
    half, count = rows // 2, 8 * rows
    a = j - (y * NX + x) * half
    b = j - count - (x * NY + y) * half + half
    same_a = (i == a) & (a >= 0) & (a < half)
    same_b = (i == b) & (b >= half) & (b < rows)
    return jnp.where(same_a | same_b, 1.0, 0.0)


def on_device(image_features, text_features, image_proj, text_proj):
    rows, width = image_features.shape
    columns = image_proj.shape[1]
    tile = (8, width)
    image_shape, text_shape = (NC, NZ, 4) + tile, (2, NY, NX, 2) + tile
    images, texts, group, unit, inverse = call(
        front_kernel,
        [image_shape, text_shape, (2, 4, rows, width), (2, rows, width), (2, rows, 128)],
        [(2, 4, rows, columns)] * 2, 1, image_features, text_features, image_proj, text_proj,
    )
    images, texts = images.reshape(-1, width), texts.reshape(-1, width)
    logits = logit_scale * dot(images, texts, ((1,), (1,))) + logit_bias
    pair_grad = jax.nn.sigmoid(logits) - pair_target(rows)
    image_sum = logit_scale * dot(pair_grad, texts, ((1,), (0,)))
    text_sum = logit_scale * dot(pair_grad, images, ((0,), (0,)))
    total_shape = (2 * columns // 8 * (width // 128), 8, 128)
    grad_image, grad_text, total = call(
        back_kernel, [(rows, width), (rows, width), total_shape], back_shapes(width, columns), 2,
        image_sum.reshape(image_shape), text_sum.reshape(text_shape), unit, inverse, group,
        image_proj, text_proj,
    )
    weights = total.reshape(2, width // 128, columns // 8, 8, 128).transpose(0, 1, 4, 2, 3)
    weights = weights.reshape(2, width, columns)
    return (grad_image, grad_text, weights[0], weights[1])


def solution(mesh):
    fine = Mesh(mesh.devices.reshape(NZ, NY, 2, 2, NC), ("z", "y", "xh", "xl", "core"))
    rows = P(("z", "y", "xh", "xl", "core"), None)
    cols = P(None, GROUP)
    return jax.shard_map(
        on_device,
        mesh=fine,
        in_specs=(rows, rows, cols, cols),
        out_specs=(rows, rows, cols, cols),
        check_vma=False,
    )
```

time: 208 us -> 170 us (0.82)
  Pallas kernels: 121 us -> 146 us
  blocking collectives: 24.5 us -> 0 us
  between operations: 14.3 us -> 0.75 us
  local copies, waits for them, and re-layouts: 19.8 us -> 10.5 us
  waiting for transfers between devices: 7.11 us -> 0 us
  other arithmetic: 4.31 us -> 0.04 us
  starting transfers between devices: 3.68 us -> 0 us
    pallas_call x3 -> x2, Pallas kernels: 121 us -> 146 us  [call(): pl.pallas_call(kernel, out_shape=[jax.ShapeDtypeStruct(s, jnp.float32) fo...]
    all_gather x2 -> x0, blocking collectives: 15.7 us -> none  [the longest x1 7.87 us: on_device(): group_image = lax.all_gather(image_features, GROUP, axis=0, tiled=True)]
    all_to_all x1 -> x0, blocking collectives: 8.75 us -> none  [on_device(): dcols = lax.all_to_all(dz, GROUP, split_axis=2, concat_axis=1, tiled=True)]
    all_to_all x1 -> x0, waiting for transfers between devices: 7.1 us -> none  [on_device(): raw = lax.all_to_all(cols, GROUP, split_axis=1, concat_axis=2, tiled=True)]
    all_to_all x6 -> x0, local copies, waits for them, and re-layouts: 5.01 us -> none  [the longest x2 2.87 us: on_device(): dcols = lax.all_to_all(dz, GROUP, split_axis=2, concat_axis=1, tiled=True)]
    another operation x5 -> x0, local copies, waits for them, and re-layouts: 4.54 us -> none  [the longest x4 3.62 us: on_device(): grad = jnp.stack(reduce_pairs(image_sum, text_sum))]
    all_to_all x1 -> x0, starting transfers between devices: 3.46 us -> none  [on_device(): raw = lax.all_to_all(cols, GROUP, split_axis=1, concat_axis=2, tiled=True)]
    slice x5 -> x3, local copies, waits for them, and re-layouts: 1.94 us -> 4.19 us  [on_device(): return (grad_image, grad_text, weights[0], weights[1])]
  transfers between devices with their start and end apart: 2 -> 0, of which waited for: 1 -> 0; matrix products, arithmetic and copies ran while one was open for 2% -> 0% of each run, Pallas kernels for 31% -> 0%
where the time goes in v3:
time: 170 us
  Pallas kernels  146 us (86%)
  matrix products  13 us (8%)
  local copies, waits for them, and re-layouts  10.5 us (6%)
    pallas_call x2, Pallas kernels, call(): pl.pallas_call(kernel, out_shape=[jax.ShapeDtypeStruct(s, jnp.float32) fo...  146 us
    dot_general x3, matrix products, dot(): lax.dot_general(a, b, (dims, ((), ())), precision=lax.Precision.HIGH, pre...  13 us
    unnamed x14, local copies, waits for them, and re-layouts  6.35 us
    slice x3, local copies, waits for them, and re-layouts, on_device(): return (grad_image, grad_text, weights[0], weights[1])  4.19 us

profile of v3, /device:TPU:8, one launch (start us, length us, event | category | flops | bytes accessed | tf_op | source)
XLA Modules:
  0.0 170.0 jit_solution(87044376429034123)
XLA Ops:
  0.6 0.0 copy-start.4
  0.7 0.0 copy-start
  0.7 0.0 copy-start.1
  0.7 3.2 %copy.8.image_w = f32[1152,288]{1,0:T(8,128)} copy(f32[1152,288]{0,1:T(8,128)} %param.6) | data formatting | bytes 2654208 | tf_op args[2]
  4.0 0.0 copy-done.4
  4.0 1.8 %copy.9.text_w = f32[1152,288]{1,0:T(8,128)} copy(f32[1152,288]{0,1:T(8,128)S(1)} %copy-done.4) | data formatting | bytes 2654208 | tf_op args[3]
  5.7 0.0 copy-done
  5.8 0.0 copy-done.1
  5.8 50.5 %shard_map.75 = (f32[2,8,4,8,1152]{4,3,2,1,0:T(8,128)}, f32[2,4,4,2,8,1152]{5,4,3,2,1,0:T(8,128)}, f32[2,4,32,1152]{3,2,1,0:T(8,128)S(1)}, f32[2,32,1152]{2,1,0:T(8,128)S(1)}, f32[2,32,128]{2,1,0:T(8,128)S(1)}) custom-call(f32[32,1152]{1,0:T(8,128)S(1)} %copy-done, f32[32,1152]{1,0:T(8,128)S(1)} %copy-done.1, f32[1152,288]{1,0:T(8,128)} %copy.8.image_w, ...), custom_call_target="tpu_custom_call" | custom-call | tf_op jit(solution)/shard_map/pallas_call | solution.py:446
  56.3 0.0 copy-start.3
  56.3 5.2 %fusion.5 = f32[512,512]{1,0:T(8,128)S(1)} fusion(f32[512,1152]{1,0:T(8,128)} %bitcast.24, f32[512,1152]{1,0:T(8,128)} %bitcast.22, s32[512]{0:T(512)S(1)} %get-tuple-element.26, s32[512]{0:T(512)S(1)} %get-tuple-element.27, s32[512]{0:T(512)S(1)} %iota_subtract_fusion.1, pred[512]{0:T(512)(128)(4,1)S(1)} %get-tuple-element.22, ...), kind=kOutput, calls=%fused_computation.8 | convolution fusion | flops 1815609344 | bytes 5775360 | tf_op jit(solution)/shard_map/dot_general | solution.py:460
  61.5 0.0 copy-done.3
  61.5 0.0 copy-start.2
  61.5 3.9 %convolution_multiply_fusion = f32[512,1152]{1,0:T(8,128)} fusion(f32[512,512]{1,0:T(8,128)S(1)} %fusion.5, f32[512,1152]{1,0:T(8,128)S(1)} %bitcast.25), kind=kOutput, calls=%fused_computation | convolution fusion | flops 1812529152 | bytes 5767168 | tf_op jit(solution)/shard_map/dot_general | solution.py:460
  65.4 0.0 copy-done.2
  65.4 3.9 %convolution_multiply_fusion.1 = f32[512,1152]{1,0:T(8,128)} fusion(f32[512,512]{1,0:T(8,128)S(1)} %fusion.5, f32[512,1152]{1,0:T(8,128)S(1)} %bitcast.23), kind=kOutput, calls=%fused_computation.1 | convolution fusion | flops 1812529152 | bytes 5767168 | tf_op jit(solution)/shard_map/dot_general | solution.py:460
  69.3 95.1 %shard_map.76 = (f32[32,1152]{1,0:T(8,128)S(1)}, f32[32,1152]{1,0:T(8,128)S(1)}, f32[648,8,128]{2,1,0:T(8,128)}) custom-call(f32[2,8,4,8,1152]{4,3,2,1,0:T(8,128)} %bitcast.20, f32[2,4,4,2,8,1152]{5,4,3,2,1,0:T(8,128)} %bitcast.19, f32[2,32,1152]{2,1,0:T(8,128)S(1)} %get-tuple-element.14.unit, f32[2,32,128]{2,1,0:T(8,128)S(1)} %get-tuple-element.15.inverse, ...), custom_call_target="tpu_custom_call" | custom-call | tf_op jit(solution)/shard_map/pallas_call | solution.py:446
  164.4 1.9 %fusion.8 = (f32[1,9,128,36,8]{2,4,3,1,0:T(8,128)S(1)}, f32[1,9,128,36,8]{2,4,3,1,0:T(8,128)S(1)}) fusion(f32[2,9,128,36,8]{2,4,3,1,0:T(8,128)} %bitcast.21), kind=kLoop, calls=%fused_computation.18 | loop fusion | bytes 5308416 | tf_op jit(solution)/shard_map/slice | solution.py:501
  166.3 1.1 copy.16
  167.5 1.1 copy.17
  168.6 0.7 copy.20
  169.3 0.7 copy.21
  (4 shorter events, 0.0 us)
Async XLA Ops:
  0.6 3.4 %copy-start.4 = (f32[1152,288]{0,1:T(8,128)S(1)}, f32[1152,288]{0,1:T(8,128)}, u32[]{:S(2)}) copy-start(f32[1152,288]{0,1:T(8,128)} %param.7) | copy-start | bytes 3981316
  0.7 5.0 %copy-start = (f32[32,1152]{1,0:T(8,128)S(1)}, f32[32,1152]{1,0:T(8,128)}, u32[]{:S(2)}) copy-start(f32[32,1152]{1,0:T(8,128)} %image_x.1) | copy-start | bytes 442372
  0.7 5.0 %copy-start.1 = (f32[32,1152]{1,0:T(8,128)S(1)}, f32[32,1152]{1,0:T(8,128)}, u32[]{:S(2)}) copy-start(f32[32,1152]{1,0:T(8,128)} %text_x.1) | copy-start | bytes 442372
  56.3 5.2 %copy-start.3 = (f32[2,8,4,8,1152]{4,3,2,1,0:T(8,128)S(1)}, f32[2,8,4,8,1152]{4,3,2,1,0:T(8,128)}, u32[]{:S(2)}) copy-start(f32[2,8,4,8,1152]{4,3,2,1,0:T(8,128)} %get-tuple-element.12) | copy-start | bytes 7077892
  61.5 3.9 %copy-start.2 = (f32[2,4,4,2,8,1152]{5,4,3,2,1,0:T(8,128)S(1)}, f32[2,4,4,2,8,1152]{5,4,3,2,1,0:T(8,128)}, u32[]{:S(2)}) copy-start(f32[2,4,4,2,8,1152]{5,4,3,2,1,0:T(8,128)} %get-tuple-element.13) | copy-start | bytes 7077892

commit v4 on v3

v4 whole, which is shorter than its diff:
```python
import functools

import jax
import jax.numpy as jnp
from jax import lax
from jax.experimental import pallas as pl
from jax.experimental.pallas import tpu as pltpu
from jax.sharding import Mesh, PartitionSpec as P

logit_scale = 100.0
logit_bias = -10.0
epsilon_norm = 1e-06
NZ, NY, NX, NC = 8, 4, 4, 2
GROUP = ("xl", "core")
MESH = pl.DeviceIdType.MESH
COPIES = 256


class Net:
    def __init__(self, send, recv):
        self.send, self.recv = send, recv
        self.z, self.y, self.c = (lax.axis_index(a) for a in ("z", "y", "core"))
        self.x = lax.axis_index("xh") * 2 + lax.axis_index("xl")
        self.started = []

    def device(self, z=None, y=None, x=None, c=None):
        z, y, x, c = (
            mine if other is None else other
            for mine, other in ((self.z, z), (self.y, y), (self.x, x), (self.c, c))
        )
        return (z, y, x // 2, x % 2, c)

    def along(self, axis, step):
        size = {"z": NZ, "y": NY, "x": NX, "c": NC}[axis]
        return self.device(**{axis: (getattr(self, axis) + step + size) % size})

    def copy(self, src, dst, device):
        k = len(self.started)
        one = pltpu.make_async_remote_copy(
            src_ref=src, dst_ref=dst, send_sem=self.send.at[k], recv_sem=self.recv.at[k],
            device_id=device, device_id_type=MESH,
        )
        one.start()
        self.started.append(one)
        return one

    def barrier(self, devices):
        semaphore = pltpu.get_barrier_semaphore()
        for device in devices:
            pl.semaphore_signal(semaphore, inc=1, device_id=device, device_id_type=MESH)
        pl.semaphore_wait(semaphore, len(devices))

    def finish(self):
        for one in self.started:
            one.wait_send()


def interleave(streams):
    streams = list(streams)
    while streams:
        left = []
        for stream in streams:
            try:
                next(stream)
                left.append(stream)
            except StopIteration:
                pass
        streams = left


def ring_gather(net, axis, n, slot, length, landed=None):
    me = getattr(net, axis)
    half = n // 2
    cut = length // 2
    parts = (pl.ds(0, cut), pl.ds(cut, length - cut))
    previous = None
    for step in range(1, half + 1):
        now = []
        for way, sign in ((0, 1), (1, -1)):
            origin = slot((me - sign * (step - 1) + n) % n)
            if previous is not None:
                previous[way].wait_recv()
            if step == half:
                origin = origin.at[parts[way]]
            now.append(net.copy(origin, origin, net.along(axis, sign)))
        if previous is not None and landed is not None:
            landed(step - 1)
            landed(1 - step)
        previous = now
        yield
    for one in previous:
        one.wait_recv()
    if landed is not None:
        landed(half)


def ring_reduce(net, axis, n, src, length, from_left, from_right, out, ready=None):
    me = getattr(net, axis)
    half = n // 2
    cut = length // 2
    parts = (pl.ds(0, cut), pl.ds(cut, length - cut))
    arrived = (from_left, from_right)
    previous = None
    for step in range(1, half + 1):
        far = half - step + 1
        now = []
        for way, sign in ((0, 1), (1, -1)):
            if ready is not None and (step > 1 or way == 0):
                ready(sign * far)
            own = src((me + sign * far + n) % n)
            if step == 1:
                piece, place = own.at[parts[way]], arrived[way].at[0, parts[way]]
            else:
                previous[way].wait_recv()
                held = arrived[way].at[step - 2]
                if step == 2:
                    held[parts[way]] = held[parts[way]] + own[parts[way]]
                    held[parts[1 - way]] = own[parts[1 - way]]
                else:
                    held[...] = held[...] + own[...]
                piece, place = held, arrived[way].at[step - 1]
            now.append(net.copy(piece, place, net.along(axis, sign)))
        previous = now
        yield
    if ready is not None:
        ready(0)
    for one in previous:
        one.wait_recv()
    out(src(me)[...] + from_left[half - 1] + from_right[half - 1])


def neighbours(net):
    return [net.along(axis, step) for axis in "zyx" for step in (1, -1)]


def group_places(net):
    low, high = net.x % 2, net.x - net.x % 2
    here = (low * 2 + net.c, low * 2 + 1 - net.c)
    there = ((1 - low) * 2 + net.c, (1 - low) * 2 + 1 - net.c)
    other = high + 1 - low
    devices = (net.device(c=1 - net.c), net.device(x=other), net.device(x=other, c=1 - net.c))
    return here + there, devices


def halves(value):
    high = value.astype(jnp.bfloat16)
    return (high, (value - high.astype(jnp.float32)).astype(jnp.bfloat16))


def dot3(a, b, dims):
    def one(p, q):
        return lax.dot_general(p, q, (dims, ((), ())), preferred_element_type=jnp.float32)

    return one(a[0], b[0]) + (one(a[0], b[1]) + one(a[1], b[0]))


A_STREAMS, B_STREAMS = 2, 2
AZ, AY = 20, 5
BY, BZ = 41, 6
A_TILES = A_STREAMS * NZ * AZ


def weight_stream_a(net, partner, base, part, total, mid, own, pair, every, z0, z1, y0, y1):
    def put(ref, index=...):
        def store(value):
            ref[index] = value

        return store

    yield from ring_reduce(
        net, "z", NZ, lambda i: part.at[pl.ds(base + i * AZ, AZ)], AZ, z0, z1, put(mid)
    )
    yield from ring_reduce(net, "y", NY, lambda i: mid.at[pl.ds(i * AY, AY)], AY, y0, y1, put(own))
    one = net.copy(own, pair, partner)
    yield
    one.wait_recv()
    every[pl.ds(net.y * AY, AY)] = own[...] + pair[...]
    yield from ring_gather(net, "y", NY, lambda i: every.at[pl.ds(i * AY, AY)], AY)
    total[pl.ds(base + net.z * AZ, AZ)] = every[...]
    yield from ring_gather(net, "z", NZ, lambda i: total.at[pl.ds(base + i * AZ, AZ)], AZ)


def weight_stream_b(net, partner, base, part, total, mid, own, pair, every, y0, y1, z0, z1):
    def put(ref, index=...):
        def store(value):
            ref[index] = value

        return store

    mid[pl.ds(BY, NZ * BZ - BY)] = jnp.zeros((NZ * BZ - BY, 8, 128), jnp.float32)
    yield from ring_reduce(
        net, "y", NY, lambda i: part.at[pl.ds(base + i * BY, BY)], BY, y0, y1, put(mid, pl.ds(0, BY))
    )
    yield from ring_reduce(net, "z", NZ, lambda i: mid.at[pl.ds(i * BZ, BZ)], BZ, z0, z1, put(own))
    one = net.copy(own, pair, partner)
    yield
    one.wait_recv()
    every[pl.ds(net.z * BZ, BZ)] = own[...] + pair[...]
    yield from ring_gather(net, "z", NZ, lambda i: every.at[pl.ds(i * BZ, BZ)], BZ)
    total[pl.ds(base + net.y * BY, BY)] = every[pl.ds(0, BY)]
    yield from ring_gather(net, "y", NY, lambda i: total.at[pl.ds(base + i * BY, BY)], BY)


def scratch_shapes(rows, width, part):
    tile, small = (8, width), (8, 128)
    full = 16 * rows
    f, h = jnp.float32, jnp.bfloat16
    shapes = {
        "w": ((2, part, width), f),
        "images": ((NC, NZ, 4) + tile, f),
        "texts": ((2, NY, NX, 2) + tile, f),
        "group": ((2, 4, rows, width), f),
        "unit": ((2, rows, width), f),
        "inverse": ((2, rows, 128), f),
        "col_out": ((2, 4, rows, part), f),
        "col_in": ((2, 4, rows, part), f),
        "image_hi": ((full, width), h),
        "image_lo": ((full, width), h),
        "text_hi": ((full, width), h),
        "text_lo": ((full, width), h),
        "image_sum": ((NC, NZ, 4) + tile, f),
        "text_sum": ((2, NY, NX, 2) + tile, f),
        "sibling": ((NZ, 4) + tile, f),
    }
    for k in range(2):
        for way in "lr":
            shapes["z%d%s" % (k, way)] = ((NZ // 2, 2) + tile, f)
    for k, (m, n) in enumerate(((NY, NX), (NX, NY))):
        shapes["t%dm" % k] = ((n, 2) + tile, f)
        for way in "lr":
            shapes["t%d1%s" % (k, way)] = ((m // 2, n, 2) + tile, f)
            shapes["t%d2%s" % (k, way)] = ((n // 2, 2) + tile, f)
    shapes["grad"] = ((2, 4) + tile, f)
    shapes["d_out"] = ((2, 4, rows, part), f)
    shapes["d_in"] = ((2, 4, rows, part), f)
    shapes["weight"] = ((part, width), f)
    shapes["terms"] = ((2 * part // 8 * (width // 128),) + small, f)
    shapes["feature"] = ((2, 4, rows, width), f)
    shapes["feature_in"] = ((2, 2, rows, width), f)
    shapes["feature_sum"] = ((2, rows, width), f)
    for k in range(A_STREAMS):
        for name, count in zip(("mid", "own", "pair", "every"), (AZ, AY, AY, AZ)):
            shapes["a%d%s" % (k, name)] = ((count,) + small, f)
        for name, shape in (("z", (NZ // 2, AZ)), ("y", (NY // 2, AY))):
            for way in "lr":
                shapes["a%d%s%s" % (k, name, way)] = (shape + small, f)
    for k in range(B_STREAMS):
        for name, count in zip(("mid", "own", "pair", "every"), (NZ * BZ, BZ, BZ, NZ * BZ)):
            shapes["b%d%s" % (k, name)] = ((count,) + small, f)
        for name, shape in (("y", (NY // 2, BY)), ("z", (NZ // 2, BZ))):
            for way in "lr":
                shapes["b%d%s%s" % (k, name, way)] = (shape + small, f)
    return shapes


def kernel(names, image_x, text_x, image_w, text_w, image_out, text_out, total, *scratch):
    s = dict(zip(names, scratch))
    send, recv, load = scratch[len(names) :]
    images, texts, group, unit, inverse = (
        s[n] for n in ("images", "texts", "group", "unit", "inverse")
    )
    net = Net(send, recv)
    (me, sib, far, diag), (to_sib, to_far, to_diag) = group_places(net)
    partner = net.device(x=(net.x + 2) % NX)
    rows, width = image_x.shape
    part = image_w.shape[0]

    loads = [pltpu.make_async_copy(w, s["w"].at[t], load.at[t]) for t, w in ((0, image_w), (1, text_w))]
    for one in loads:
        one.start()
    group[0, me] = image_x[...]
    group[1, me] = text_x[...]
    net.barrier(neighbours(net) + [to_sib, to_diag, partner])

    first = []
    for t in range(2):
        block = group.at[t, me]
        first.append((net.copy(block, block, to_far), net.copy(block, block, to_sib)))
    across = []

    def prepare(t):
        loads[t].wait()
        weights = halves(s["w"][t])
        first[t][0].wait_recv()
        block = group.at[t, far]
        onward = net.copy(block, block, to_sib)
        yield
        first[t][1].wait_recv()
        onward.wait_recv()
        cols = dot3(halves(group[t].reshape(4 * rows, width)), weights, ((1,), (1,)))
        s["col_out"][t] = cols.reshape(4, rows, part)
        copies = [
            net.copy(s["col_out"].at[t, place], s["col_in"].at[t, me], device)
            for place, device in ((far, to_far), (diag, to_diag), (sib, to_sib))
        ]
        s["col_in"][t, me] = s["col_out"][t, me]
        yield
        for one in copies:
            one.wait_recv()
        raw = jnp.concatenate([s["col_in"][t, k] for k in range(4)], axis=1)
        scale = lax.rsqrt(jnp.sum(raw * raw, axis=1, keepdims=True) + epsilon_norm)
        unit[t] = raw * scale
        inverse[t] = jnp.broadcast_to(scale, (rows, 128))

    def image_start():
        yield from prepare(0)
        images[net.c, net.z] = unit[0].reshape(4, 8, width)

    def text_start():
        yield from prepare(1)
        tiles = unit[1].reshape(4, 8, width)
        texts[0, net.y, net.x] = tiles[0:2]
        texts[1, net.x, net.y] = tiles[2:4]

    def image_gather(first, length):
        def slot(z):
            return images.at[net.c, z, pl.ds(first, length)]

        def landed(relative):
            block = slot((net.z + relative + NZ) % NZ)
            across.append(net.copy(block, block, to_sib))

        yield from ring_gather(net, "z", NZ, slot, length, landed)

    def text_gather(half, first, second, counts):
        buffer = texts.at[half]
        row = buffer.at[getattr(net, second)]
        yield from ring_gather(net, first, counts[0], lambda i: row.at[i], 2)
        yield from ring_gather(net, second, counts[1], lambda i: buffer.at[i], counts[0])

    interleave([image_start(), text_start()])
    own = images.at[net.c, net.z]
    streams = [
        image_gather(0, 2),
        text_gather(0, "x", "y", (NX, NY)),
        text_gather(1, "y", "x", (NY, NX)),
        image_gather(2, 2),
    ]
    for stream in streams:
        next(stream)
    across.append(net.copy(own, own, to_sib))
    interleave(streams)
    for one in across:
        one.wait_recv()

    full = 16 * rows
    eighth = full // 8

    def split(i, carry):
        where = pl.ds(pl.multiple_of(i * eighth, eighth), eighth)
        high, low = halves(texts[i // 4, i % 4].reshape(eighth, width))
        s["text_hi"][where] = high
        s["text_lo"][where] = low
        high, low = halves(images[i // 4, pl.ds((i % 4) * 2, 2)].reshape(eighth, width))
        s["image_hi"][where] = high
        s["image_lo"][where] = low
        return carry

    lax.fori_loop(0, 8, split, 0)
    text_halves = (s["text_hi"], s["text_lo"])
    count = full // 2
    pending = {}
    for turn, c in enumerate((1 - net.c, net.c)):
        where = pl.ds(pl.multiple_of(c * count, count), count)
        image_block = (s["image_hi"][where], s["image_lo"][where])
        pair = tuple(r[...] for r in text_halves)
        logits = logit_scale * dot3(image_block, pair, ((1,), (1,))) + logit_bias
        grad_block = halves(jax.nn.sigmoid(logits) - pair_target(net, rows, c, count))
        s["image_sum"][c] = (logit_scale * dot3(grad_block, pair, ((1,), (0,)))).reshape(
            NZ, 4, 8, width
        )
        if turn == 0:
            for relative in (4, 3, -3, 2, -2, 1, -1, 0):
                z = (net.z + relative + NZ) % NZ
                pending[relative] = net.copy(
                    s["image_sum"].at[c, z], s["sibling"].at[z], to_sib
                )
        text_term = (logit_scale * dot3(grad_block, image_block, ((0,), (0,)))).reshape(
            2, NY, NX, 2, 8, width
        )
        if turn == 0:
            s["text_sum"][...] = text_term
        else:
            s["text_sum"][...] = s["text_sum"][...] + text_term

    summed = set()

    def ready(relative):
        if relative in summed:
            return
        summed.add(relative)
        z = (net.z + relative + NZ) % NZ
        pending[relative].wait_recv()
        s["sibling"][z] = s["sibling"][z] + s["image_sum"][net.c, z]

    def put(ref, *index):
        def store(value):
            ref[index] = value

        return store

    def image_reduce(k):
        where = pl.ds(2 * k, 2)
        yield from ring_reduce(
            net, "z", NZ, lambda i: s["sibling"].at[i, where], 2,
            s["z%dl" % k], s["z%dr" % k], put(s["grad"], 0, where), ready,
        )

    def text_reduce(k, first, second, counts):
        buffer, middle = s["text_sum"].at[k], s["t%dm" % k]
        yield from ring_reduce(
            net, first, counts[0], lambda i: buffer.at[i], counts[1],
            s["t%d1l" % k], s["t%d1r" % k], put(middle, ...),
        )
        yield from ring_reduce(
            net, second, counts[1], lambda i: middle.at[i], 2,
            s["t%d2l" % k], s["t%d2r" % k], put(s["grad"], 1, pl.ds(2 * k, 2)),
        )

    interleave(
        [
            text_reduce(0, "y", "x", (NY, NX)),
            text_reduce(1, "x", "y", (NX, NY)),
            image_reduce(0),
            image_reduce(1),
        ]
    )

    d_out, d_in, feature = s["d_out"], s["d_in"], s["feature"]
    exchanged = []
    for t in range(2):
        g, u = s["grad"][t].reshape(rows, width), unit[t]
        dz = inverse[t][:, :1] * (g - u * jnp.sum(u * g, axis=1, keepdims=True))
        for k in range(4):
            d_out[t, k] = dz[:, k * part : (k + 1) * part]
        exchanged.append(
            [
                net.copy(d_out.at[t, place], d_in.at[t, me], device)
                for place, device in ((far, to_far), (diag, to_diag), (sib, to_sib))
            ]
        )
        d_in[t, me] = d_out[t, me]

    lanes = width // 128
    terms, weight = s["terms"], s["weight"]

    def weight_terms(t):
        for one in exchanged[t]:
            one.wait_recv()
        dcols = halves(d_in[t].reshape(4 * rows, part))
        weight[...] = dot3(dcols, halves(group[t].reshape(4 * rows, width)), ((0,), (0,)))
        base = t * (part // 8) * lanes

        def retile(r, carry):
            strip = weight[pl.ds(pl.multiple_of(r * 8, 8), 8)]
            for j in range(lanes):
                terms[base + r * lanes + j] = strip[:, j * 128 : (j + 1) * 128]
            return carry

        lax.fori_loop(0, part // 8, retile, 0)

    def feature_stream():
        first = []
        for t in range(2):
            dcols = halves(d_in[t].reshape(4 * rows, part))
            feature[t] = dot3(dcols, halves(s["w"][t]), ((1,), (0,))).reshape(4, rows, width)
            first.append(
                (
                    net.copy(feature.at[t, diag], s["feature_in"].at[t, 0], to_sib),
                    net.copy(feature.at[t, sib], s["feature_in"].at[t, 1], to_sib),
                )
            )
        yield
        last = []
        for t in range(2):
            first[t][0].wait_recv()
            s["feature_in"][t, 0] = s["feature_in"][t, 0] + feature[t, far]
            last.append(net.copy(s["feature_in"].at[t, 0], s["feature_sum"].at[t], to_far))
        for _ in range(6):
            yield
        for t, out in ((0, image_out), (1, text_out)):
            first[t][1].wait_recv()
            last[t].wait_recv()
            out[...] = feature[t, me] + s["feature_in"][t, 1] + s["feature_sum"][t]

    def pick(prefix, *names):
        return [s[prefix + n] for n in names]

    stream_a = [
        weight_stream_a(
            net, partner, k * NZ * AZ, terms, total,
            *pick("a%d" % k, "mid", "own", "pair", "every", "zl", "zr", "yl", "yr"),
        )
        for k in range(A_STREAMS)
    ]
    stream_b = [
        weight_stream_b(
            net, partner, A_TILES + k * NY * BY, terms, total,
            *pick("b%d" % k, "mid", "own", "pair", "every", "yl", "yr", "zl", "zr"),
        )
        for k in range(B_STREAMS)
    ]
    weight_terms(0)
    for one in stream_a:
        next(one)
    weight_terms(1)
    for one in stream_b:
        next(one)
    order = [stream for pair in zip(stream_a, stream_b) for stream in pair]
    interleave([feature_stream()] + order)
    net.finish()


def pair_target(net, rows, core, count):
    i = lax.broadcasted_iota(jnp.int32, (count, 16 * rows), 0) + (core - net.c) * count
    i = i - net.z * rows
    j = lax.broadcasted_iota(jnp.int32, (count, 16 * rows), 1)
    half = rows // 2
    a = j - (net.y * NX + net.x) * half
    b = j - 8 * rows - (net.x * NY + net.y) * half + half
    same_a = (i == a) & (a >= 0) & (a < half)
    same_b = (i == b) & (b >= half) & (b < rows)
    return jnp.where(same_a | same_b, 1.0, 0.0)


def on_device(image_features, text_features, image_proj, text_proj):
    rows, width = image_features.shape
    part = image_proj.shape[1]
    shapes = scratch_shapes(rows, width, part)
    total_shape = (2 * part // 8 * (width // 128), 8, 128)
    vmem = pl.BlockSpec(memory_space=pltpu.VMEM)
    anywhere = pl.BlockSpec(memory_space=pl.ANY)
    semaphores = [pltpu.SemaphoreType.DMA((n,)) for n in (COPIES, COPIES, 2)]
    grad_image, grad_text, total = pl.pallas_call(
        functools.partial(kernel, tuple(shapes)),
        out_shape=[
            jax.ShapeDtypeStruct(shape, jnp.float32)
            for shape in ((rows, width), (rows, width), total_shape)
        ],
        in_specs=[vmem, vmem, anywhere, anywhere],
        out_specs=[vmem] * 3,
        scratch_shapes=[pltpu.VMEM(shape, kind) for shape, kind in shapes.values()] + semaphores,
        compiler_params=pltpu.CompilerParams(
            collective_id=1, has_side_effects=True, vmem_limit_bytes=60 * 2**20
        ),
    )(image_features, text_features, image_proj.T, text_proj.T)
    weights = total.reshape(2, part // 8, width // 128, 8, 128).transpose(0, 1, 3, 2, 4)
    weights = weights.reshape(2, part, width)
    return (grad_image, grad_text, weights[0].T, weights[1].T)


def solution(mesh):
    fine = Mesh(mesh.devices.reshape(NZ, NY, 2, 2, NC), ("z", "y", "xh", "xl", "core"))
    rows = P(("z", "y", "xh", "xl", "core"), None)
    cols = P(None, GROUP)
    return jax.shard_map(
        on_device,
        mesh=fine,
        in_specs=(rows, rows, cols, cols),
        out_specs=(rows, rows, cols, cols),
        check_vma=False,
    )
```

time: 170 us -> 152 us (0.89)
  matrix products: 13 us -> 0 us
  local copies, waits for them, and re-layouts: 10.5 us -> 4.77 us
    dot_general x3 -> x0, matrix products: 13 us -> none  [dot(): lax.dot_general(a, b, (dims, ((), ())), precision=lax.Precision.HIGH, pre...]
    unnamed x14 -> x6, local copies, waits for them, and re-layouts: 6.35 us -> 1.33 us
    slice x3 -> x0, local copies, waits for them, and re-layouts: 4.19 us -> none  [on_device(): return (grad_image, grad_text, weights[0], weights[1])]
    transpose x0 -> x1, local copies, waits for them, and re-layouts: none -> 3.44 us  [on_device(): return (grad_image, grad_text, weights[0].T, weights[1].T)]
    pallas_call x2 -> x1, Pallas kernels: 146 us -> 146 us  [on_device(): pl.pallas_call(functools.partial(kernel, tuple(shapes)), out_shape=[jax.S...]
where the time goes in v4:
time: 152 us; the launch traced here: 151 us
  Pallas kernels  146 us (96%)
  local copies, waits for them, and re-layouts  4.77 us (3%)
    pallas_call x1, Pallas kernels, on_device(): pl.pallas_call(functools.partial(kernel, tuple(shapes)), out_shape=[jax.S...  146 us
    transpose x1, local copies, waits for them, and re-layouts, on_device(): return (grad_image, grad_text, weights[0].T, weights[1].T)  3.44 us

profile of v4, /device:TPU:8, one launch (start us, length us, event | category | flops | bytes accessed | tf_op | source)
XLA Modules:
  0.0 151.5 jit_solution(14046578648432786922)
XLA Ops:
  0.6 146.1 %shard_map.75 = (f32[32,1152]{1,0:T(8,128)}, f32[32,1152]{1,0:T(8,128)}, f32[648,8,128]{2,1,0:T(8,128)}) custom-call(f32[32,1152]{1,0:T(8,128)} %image_x.1, f32[32,1152]{1,0:T(8,128)} %text_x.1, f32[288,1152]{1,0:T(8,128)} %bitcast.14, f32[288,1152]{1,0:T(8,128)} %bitcast.15), custom_call_target="tpu_custom_call" | custom-call | tf_op jit(solution)/shard_map/pallas_call | solution.py:534
  146.7 0.0 copy-start.1
  146.7 0.0 copy-start
  146.7 3.4 %slice_bitcast_fusion = (f32[1152,288]{0,1:T(8,128)}, f32[1152,288]{0,1:T(8,128)}) fusion(f32[2,36,8,9,128]{4,2,3,1,0:T(8,128)} %bitcast.13), kind=kLoop, calls=%fused_computation | loop fusion | bytes 5308416 | tf_op jit(solution)/shard_map/transpose | solution.py:549
  150.2 0.0 copy-done.1
  150.2 0.7 copy.10
  150.8 0.0 copy-done
  150.8 0.7 copy.11
Async XLA Ops:
  146.7 3.5 %copy-start.1 = (f32[32,1152]{1,0:T(8,128)S(1)}, f32[32,1152]{1,0:T(8,128)}, u32[]{:S(2)}) copy-start(f32[32,1152]{1,0:T(8,128)} %get-tuple-element.16) | copy-start | bytes 442372
  146.7 4.1 %copy-start = (f32[32,1152]{1,0:T(8,128)S(1)}, f32[32,1152]{1,0:T(8,128)}, u32[]{:S(2)}) copy-start(f32[32,1152]{1,0:T(8,128)} %get-tuple-element.17) | copy-start | bytes 442372

commit v5 on v4

--- a/solution.py
+++ b/solution.py
@@ -1,4 +1,5 @@
 import functools
+import math
 
 import jax
 import jax.numpy as jnp
@@ -13,7 +14,15 @@
 NZ, NY, NX, NC = 8, 4, 4, 2
 GROUP = ("xl", "core")
 MESH = pl.DeviceIdType.MESH
-COPIES = 256
+COPIES = 320
+LINK_RATE, LINK_DELAY = 45e3, 2.0
+CORE_RATE, CORE_DELAY = 350e3, 1.0
+
+
+class Flight:
+    def __init__(self, copy, due):
+        self.copy, self.due = copy, due
+        self.wait_recv, self.wait_send = copy.wait_recv, copy.wait_send
 
 
 class Net:
@@ -22,6 +31,10 @@
         self.z, self.y, self.c = (lax.axis_index(a) for a in ("z", "y", "core"))
         self.x = lax.axis_index("xh") * 2 + lax.axis_index("xl")
         self.started = []
+        self.now = 0.0
+        self.free = {}
+        self.queue = []
+        self.spawned = 0
 
     def device(self, z=None, y=None, x=None, c=None):
         z, y, x, c = (
@@ -34,15 +47,27 @@
         size = {"z": NZ, "y": NY, "x": NX, "c": NC}[axis]
         return self.device(**{axis: (getattr(self, axis) + step + size) % size})
 
-    def copy(self, src, dst, device):
+    def copy(self, src, dst, device, link=None):
         k = len(self.started)
         one = pltpu.make_async_remote_copy(
             src_ref=src, dst_ref=dst, send_sem=self.send.at[k], recv_sem=self.recv.at[k],
             device_id=device, device_id_type=MESH,
         )
         one.start()
+        size = 4.0 * math.prod(src.shape)
+        if link is None:
+            due = self.now + size / CORE_RATE + CORE_DELAY
+        else:
+            left = max(self.now, self.free.get(link, 0.0)) + size / LINK_RATE
+            self.free[link] = left
+            due = left + LINK_DELAY
+        one = Flight(one, due)
         self.started.append(one)
         return one
+
+    def spawn(self, stream, due=0.0):
+        self.queue.append((max(self.now, due), self.spawned, stream))
+        self.spawned += 1
 
     def barrier(self, devices):
         semaphore = pltpu.get_barrier_semaphore()
@@ -51,21 +76,22 @@
         pl.semaphore_wait(semaphore, len(devices))
 
     def finish(self):
+        assert len(self.started) <= COPIES
         for one in self.started:
             one.wait_send()
 
 
-def interleave(streams):
-    streams = list(streams)
-    while streams:
-        left = []
-        for stream in streams:
-            try:
-                next(stream)
-                left.append(stream)
-            except StopIteration:
-                pass
-        streams = left
+def interleave(net, streams):
+    for stream in streams:
+        net.spawn(stream)
+    while net.queue:
+        turn = min(net.queue, key=lambda entry: entry[:2])
+        net.queue.remove(turn)
+        due, k, stream = turn
+        net.now = max(net.now, due)
+        due = next(stream, None)
+        if due is not None:
+            net.queue.append((due, k, stream))
 
 
 def ring_gather(net, axis, n, slot, length, landed=None):
@@ -82,12 +108,12 @@
                 previous[way].wait_recv()
             if step == half:
                 origin = origin.at[parts[way]]
-            now.append(net.copy(origin, origin, net.along(axis, sign)))
+            now.append(net.copy(origin, origin, net.along(axis, sign), (axis, sign)))
         if previous is not None and landed is not None:
             landed(step - 1)
             landed(1 - step)
         previous = now
-        yield
+        yield max(one.due for one in now)
     for one in previous:
         one.wait_recv()
     if landed is not None:
@@ -105,8 +131,8 @@
         far = half - step + 1
         now = []
         for way, sign in ((0, 1), (1, -1)):
-            if ready is not None and (step > 1 or way == 0):
-                ready(sign * far)
+            while ready is not None and not ready(sign * far):
+                yield net.now + 0.3
             own = src((me + sign * far + n) % n)
             if step == 1:
                 piece, place = own.at[parts[way]], arrived[way].at[0, parts[way]]
@@ -119,11 +145,11 @@
                 else:
                     held[...] = held[...] + own[...]
                 piece, place = held, arrived[way].at[step - 1]
-            now.append(net.copy(piece, place, net.along(axis, sign)))
+            now.append(net.copy(piece, place, net.along(axis, sign), (axis, sign)))
         previous = now
-        yield
-    if ready is not None:
-        ready(0)
+        yield max(one.due for one in now)
+    while ready is not None and not ready(0):
+        yield net.now + 0.3
     for one in previous:
         one.wait_recv()
     out(src(me)[...] + from_left[half - 1] + from_right[half - 1])
@@ -155,27 +181,41 @@
 
 
 A_STREAMS, B_STREAMS = 2, 2
-AZ, AY = 20, 5
-BY, BZ = 41, 6
-A_TILES = A_STREAMS * NZ * AZ
-
-
-def weight_stream_a(net, partner, base, part, total, mid, own, pair, every, z0, z1, y0, y1):
-    def put(ref, index=...):
-        def store(value):
-            ref[index] = value
-
-        return store
+AZ, AY = 16, 2
+BY, BZ = 49, 7
+B_TILES = B_STREAMS * NY * BY
+
+
+def weight_stream_a(net, base, part, total, mid, others, every, z0, z1):
+    def store(value):
+        mid[...] = value
 
     yield from ring_reduce(
-        net, "z", NZ, lambda i: part.at[pl.ds(base + i * AZ, AZ)], AZ, z0, z1, put(mid)
+        net, "z", NZ, lambda i: part.at[pl.ds(base + i * AZ, AZ)], AZ, z0, z1, store
     )
-    yield from ring_reduce(net, "y", NY, lambda i: mid.at[pl.ds(i * AY, AY)], AY, y0, y1, put(own))
-    one = net.copy(own, pair, partner)
-    yield
-    one.wait_recv()
-    every[pl.ds(net.y * AY, AY)] = own[...] + pair[...]
-    yield from ring_gather(net, "y", NY, lambda i: every.at[pl.ds(i * AY, AY)], AY)
+    high = net.x // 2
+    mine = pl.ds((net.y * 2 + high) * AY, AY)
+    peers = []
+    for k in range(1, 2 * NY):
+        y, h = (net.y + k // 2) % NY, (high + k % 2) % 2
+        peers.append((pl.ds((y * 2 + h) * AY, AY), net.device(y=y, x=h * 2 + net.x % 2)))
+    copies = [
+        net.copy(mid.at[chunk], others.at[k], device, ("y", 1))
+        for k, (chunk, device) in enumerate(peers)
+    ]
+    yield copies[-1].due
+    for one in copies:
+        one.wait_recv()
+    value = mid[mine]
+    for k in range(len(peers)):
+        value = value + others[k]
+    every[mine] = value
+    copies = [
+        net.copy(every.at[mine], every.at[mine], device, ("y", 1)) for _, device in peers
+    ]
+    yield copies[-1].due
+    for one in copies:
+        one.wait_recv()
     total[pl.ds(base + net.z * AZ, AZ)] = every[...]
     yield from ring_gather(net, "z", NZ, lambda i: total.at[pl.ds(base + i * AZ, AZ)], AZ)
 
@@ -192,8 +232,8 @@
         net, "y", NY, lambda i: part.at[pl.ds(base + i * BY, BY)], BY, y0, y1, put(mid, pl.ds(0, BY))
     )
     yield from ring_reduce(net, "z", NZ, lambda i: mid.at[pl.ds(i * BZ, BZ)], BZ, z0, z1, put(own))
-    one = net.copy(own, pair, partner)
-    yield
+    one = net.copy(own, pair, partner, ("x", 2))
+    yield one.due + 1.0
     one.wait_recv()
     every[pl.ds(net.z * BZ, BZ)] = own[...] + pair[...]
     yield from ring_gather(net, "z", NZ, lambda i: every.at[pl.ds(i * BZ, BZ)], BZ)
@@ -218,6 +258,8 @@
         "image_lo": ((full, width), h),
         "text_hi": ((full, width), h),
         "text_lo": ((full, width), h),
+        "pair_hi": ((full, full), h),
+        "pair_lo": ((full, full), h),
         "image_sum": ((NC, NZ, 4) + tile, f),
         "text_sum": ((2, NY, NX, 2) + tile, f),
         "sibling": ((NZ, 4) + tile, f),
@@ -228,7 +270,7 @@
     for k, (m, n) in enumerate(((NY, NX), (NX, NY))):
         shapes["t%dm" % k] = ((n, 2) + tile, f)
         for way in "lr":
-            shapes["t%d1%s" % (k, way)] = ((m // 2, n, 2) + tile, f)
+            shapes["t%d1%s" % (k, way)] = ((n, m // 2, 2) + tile, f)
             shapes["t%d2%s" % (k, way)] = ((n // 2, 2) + tile, f)
     shapes["grad"] = ((2, 4) + tile, f)
     shapes["d_out"] = ((2, 4, rows, part), f)
@@ -239,11 +281,11 @@
     shapes["feature_in"] = ((2, 2, rows, width), f)
     shapes["feature_sum"] = ((2, rows, width), f)
     for k in range(A_STREAMS):
-        for name, count in zip(("mid", "own", "pair", "every"), (AZ, AY, AY, AZ)):
-            shapes["a%d%s" % (k, name)] = ((count,) + small, f)
-        for name, shape in (("z", (NZ // 2, AZ)), ("y", (NY // 2, AY))):
-            for way in "lr":
-                shapes["a%d%s%s" % (k, name, way)] = (shape + small, f)
+        shapes["a%dmid" % k] = ((AZ,) + small, f)
+        shapes["a%dothers" % k] = ((2 * NY - 1, AY) + small, f)
+        shapes["a%devery" % k] = ((AZ,) + small, f)
+        for way in "lr":
+            shapes["a%dz%s" % (k, way)] = ((NZ // 2, AZ) + small, f)
     for k in range(B_STREAMS):
         for name, count in zip(("mid", "own", "pair", "every"), (NZ * BZ, BZ, BZ, NZ * BZ)):
             shapes["b%d%s" % (k, name)] = ((count,) + small, f)
@@ -270,12 +312,16 @@
         one.start()
     group[0, me] = image_x[...]
     group[1, me] = text_x[...]
-    net.barrier(neighbours(net) + [to_sib, to_diag, partner])
+    column = [
+        net.device(y=(net.y + dy) % NY, x=(net.x + dx) % NX)
+        for dy in range(NY) for dx in (0, 2) if dy == 2 or dx == 2
+    ]
+    net.barrier(neighbours(net) + [to_sib, to_diag] + column)
 
     first = []
     for t in range(2):
         block = group.at[t, me]
-        first.append((net.copy(block, block, to_far), net.copy(block, block, to_sib)))
+        first.append((net.copy(block, block, to_far, ("x", 0)), net.copy(block, block, to_sib)))
     across = []
 
     def prepare(t):
@@ -284,7 +330,7 @@
         first[t][0].wait_recv()
         block = group.at[t, far]
         onward = net.copy(block, block, to_sib)
-        yield
+        yield onward.due
         first[t][1].wait_recv()
         onward.wait_recv()
         cols = dot3(halves(group[t].reshape(4 * rows, width)), weights, ((1,), (1,)))
@@ -294,7 +340,7 @@
             for place, device in ((far, to_far), (diag, to_diag), (sib, to_sib))
         ]
         s["col_in"][t, me] = s["col_out"][t, me]
-        yield
+        yield copies[0].due
         for one in copies:
             one.wait_recv()
         raw = jnp.concatenate([s["col_in"][t, k] for k in range(4)], axis=1)
@@ -305,12 +351,18 @@
     def image_start():
         yield from prepare(0)
         images[net.c, net.z] = unit[0].reshape(4, 8, width)
+        for k in range(2):
+            net.spawn(image_gather(2 * k, 2))
+        own = images.at[net.c, net.z]
+        across.append(net.copy(own, own, to_sib))
 
     def text_start():
         yield from prepare(1)
         tiles = unit[1].reshape(4, 8, width)
         texts[0, net.y, net.x] = tiles[0:2]
         texts[1, net.x, net.y] = tiles[2:4]
+        net.spawn(text_gather(0, "x", "y", (NX, NY)))
+        net.spawn(text_gather(1, "y", "x", (NY, NX)))
 
     def image_gather(first, length):
         def slot(z):
@@ -325,21 +377,18 @@
     def text_gather(half, first, second, counts):
         buffer = texts.at[half]
         row = buffer.at[getattr(net, second)]
-        yield from ring_gather(net, first, counts[0], lambda i: row.at[i], 2)
-        yield from ring_gather(net, second, counts[1], lambda i: buffer.at[i], counts[0])
-
-    interleave([image_start(), text_start()])
-    own = images.at[net.c, net.z]
-    streams = [
-        image_gather(0, 2),
-        text_gather(0, "x", "y", (NX, NY)),
-        text_gather(1, "y", "x", (NY, NX)),
-        image_gather(2, 2),
-    ]
-    for stream in streams:
-        next(stream)
-    across.append(net.copy(own, own, to_sib))
-    interleave(streams)
+
+        def landed(relative):
+            i = (getattr(net, first) + relative + counts[0]) % counts[0]
+            net.spawn(ring_gather(net, second, counts[1], lambda j: buffer.at[j, i], 2))
+
+        stream = ring_gather(net, first, counts[0], lambda i: row.at[i], 2, landed)
+        due = next(stream)
+        landed(0)
+        yield due
+        yield from stream
+
+    interleave(net, [image_start(), text_start()])
     for one in across:
         one.wait_recv()
 
@@ -365,8 +414,10 @@
         image_block = (s["image_hi"][where], s["image_lo"][where])
         pair = tuple(r[...] for r in text_halves)
         logits = logit_scale * dot3(image_block, pair, ((1,), (1,))) + logit_bias
-        grad_block = halves(jax.nn.sigmoid(logits) - pair_target(net, rows, c, count))
-        s["image_sum"][c] = (logit_scale * dot3(grad_block, pair, ((1,), (0,)))).reshape(
+        high, low = halves(jax.nn.sigmoid(logits) - pair_target(net, rows, c, count))
+        s["pair_hi"][where] = high
+        s["pair_lo"][where] = low
+        s["image_sum"][c] = (logit_scale * dot3((high, low), pair, ((1,), (0,)))).reshape(
             NZ, 4, 8, width
         )
         if turn == 0:
@@ -375,23 +426,18 @@
                 pending[relative] = net.copy(
                     s["image_sum"].at[c, z], s["sibling"].at[z], to_sib
                 )
-        text_term = (logit_scale * dot3(grad_block, image_block, ((0,), (0,)))).reshape(
-            2, NY, NX, 2, 8, width
-        )
-        if turn == 0:
-            s["text_sum"][...] = text_term
-        else:
-            s["text_sum"][...] = s["text_sum"][...] + text_term
 
     summed = set()
 
     def ready(relative):
+        relative = relative if relative != -NZ // 2 else NZ // 2
         if relative in summed:
-            return
+            return True
         summed.add(relative)
         z = (net.z + relative + NZ) % NZ
         pending[relative].wait_recv()
         s["sibling"][z] = s["sibling"][z] + s["image_sum"][net.c, z]
+        return True
 
     def put(ref, *index):
         def store(value):
@@ -408,45 +454,33 @@
 
     def text_reduce(k, first, second, counts):
         buffer, middle = s["text_sum"].at[k], s["t%dm" % k]
-        yield from ring_reduce(
-            net, first, counts[0], lambda i: buffer.at[i], counts[1],
-            s["t%d1l" % k], s["t%d1r" % k], put(middle, ...),
-        )
+        finished = set()
+
+        def ready(relative):
+            return relative % counts[1] in finished
+
+        def strip(relative):
+            i = (getattr(net, second) + relative) % counts[1]
+            yield from ring_reduce(
+                net, first, counts[0], lambda j: buffer.at[j, i], 2,
+                s["t%d1l" % k].at[relative], s["t%d1r" % k].at[relative], put(middle, i),
+            )
+            finished.add(relative)
+
+        for relative in (2, 1, 3, 0):
+            net.spawn(strip(relative))
+        yield net.now + 5.0
         yield from ring_reduce(
             net, second, counts[1], lambda i: middle.at[i], 2,
-            s["t%d2l" % k], s["t%d2r" % k], put(s["grad"], 1, pl.ds(2 * k, 2)),
+            s["t%d2l" % k], s["t%d2r" % k], put(s["grad"], 1, pl.ds(2 * k, 2)), ready,
         )
 
-    interleave(
-        [
-            text_reduce(0, "y", "x", (NY, NX)),
-            text_reduce(1, "x", "y", (NX, NY)),
-            image_reduce(0),
-            image_reduce(1),
-        ]
-    )
-
     d_out, d_in, feature = s["d_out"], s["d_in"], s["feature"]
-    exchanged = []
-    for t in range(2):
-        g, u = s["grad"][t].reshape(rows, width), unit[t]
-        dz = inverse[t][:, :1] * (g - u * jnp.sum(u * g, axis=1, keepdims=True))
-        for k in range(4):
-            d_out[t, k] = dz[:, k * part : (k + 1) * part]
-        exchanged.append(
-            [
-                net.copy(d_out.at[t, place], d_in.at[t, me], device)
-                for place, device in ((far, to_far), (diag, to_diag), (sib, to_sib))
-            ]
-        )
-        d_in[t, me] = d_out[t, me]
 
     lanes = width // 128
     terms, weight = s["terms"], s["weight"]
 
     def weight_terms(t):
-        for one in exchanged[t]:
-            one.wait_recv()
         dcols = halves(d_in[t].reshape(4 * rows, part))
         weight[...] = dot3(dcols, halves(group[t].reshape(4 * rows, width)), ((0,), (0,)))
         base = t * (part // 8) * lanes
@@ -459,55 +493,85 @@
 
         lax.fori_loop(0, part // 8, retile, 0)
 
-    def feature_stream():
-        first = []
-        for t in range(2):
-            dcols = halves(d_in[t].reshape(4 * rows, part))
-            feature[t] = dot3(dcols, halves(s["w"][t]), ((1,), (0,))).reshape(4, rows, width)
-            first.append(
-                (
-                    net.copy(feature.at[t, diag], s["feature_in"].at[t, 0], to_sib),
-                    net.copy(feature.at[t, sib], s["feature_in"].at[t, 1], to_sib),
-                )
-            )
-        yield
-        last = []
-        for t in range(2):
-            first[t][0].wait_recv()
-            s["feature_in"][t, 0] = s["feature_in"][t, 0] + feature[t, far]
-            last.append(net.copy(s["feature_in"].at[t, 0], s["feature_sum"].at[t], to_far))
-        for _ in range(6):
-            yield
-        for t, out in ((0, image_out), (1, text_out)):
-            first[t][1].wait_recv()
-            last[t].wait_recv()
-            out[...] = feature[t, me] + s["feature_in"][t, 1] + s["feature_sum"][t]
+    def feature_stream(t, out):
+        dcols = halves(d_in[t].reshape(4 * rows, part))
+        feature[t] = dot3(dcols, halves(s["w"][t]), ((1,), (0,))).reshape(4, rows, width)
+        net.now += 1.0
+        onward = net.copy(feature.at[t, diag], s["feature_in"].at[t, 0], to_sib)
+        near = net.copy(feature.at[t, sib], s["feature_in"].at[t, 1], to_sib)
+        yield near.due
+        onward.wait_recv()
+        s["feature_in"][t, 0] = s["feature_in"][t, 0] + feature[t, far]
+        last = net.copy(s["feature_in"].at[t, 0], s["feature_sum"].at[t], to_far, ("x", 0))
+        yield last.due + 8.0
+        near.wait_recv()
+        last.wait_recv()
+        out[...] = feature[t, me] + s["feature_in"][t, 1] + s["feature_sum"][t]
 
     def pick(prefix, *names):
         return [s[prefix + n] for n in names]
 
-    stream_a = [
-        weight_stream_a(
-            net, partner, k * NZ * AZ, terms, total,
-            *pick("a%d" % k, "mid", "own", "pair", "every", "zl", "zr", "yl", "yr"),
+    def stream_a(k):
+        return weight_stream_a(
+            net, B_TILES + k * NZ * AZ, terms, total,
+            *pick("a%d" % k, "mid", "others", "every", "zl", "zr"),
         )
-        for k in range(A_STREAMS)
-    ]
-    stream_b = [
-        weight_stream_b(
-            net, partner, A_TILES + k * NY * BY, terms, total,
+
+    def stream_b(k):
+        return weight_stream_b(
+            net, partner, k * NY * BY, terms, total,
             *pick("b%d" % k, "mid", "own", "pair", "every", "yl", "yr", "zl", "zr"),
         )
-        for k in range(B_STREAMS)
-    ]
-    weight_terms(0)
-    for one in stream_a:
-        next(one)
-    weight_terms(1)
-    for one in stream_b:
-        next(one)
-    order = [stream for pair in zip(stream_a, stream_b) for stream in pair]
-    interleave([feature_stream()] + order)
+
+    def in_turn(streams):
+        for stream in streams:
+            due = next(stream)
+            net.spawn(stream, due)
+            yield due
+
+    def tower(t, out, streams):
+        g, u = s["grad"][t].reshape(rows, width), unit[t]
+        dz = inverse[t][:, :1] * (g - u * jnp.sum(u * g, axis=1, keepdims=True))
+        for k in range(4):
+            d_out[t, k] = dz[:, k * part : (k + 1) * part]
+        copies = [
+            net.copy(d_out.at[t, place], d_in.at[t, me], device, link)
+            for place, device, link in ((far, to_far, ("x", 0)), (diag, to_diag, ("x", 0)), (sib, to_sib, None))
+        ]
+        d_in[t, me] = d_out[t, me]
+        yield copies[1].due
+        for one in copies:
+            one.wait_recv()
+        weight_terms(t)
+        net.now += 1.0
+        for several in streams:
+            net.spawn(in_turn(several))
+        net.spawn(feature_stream(t, out), net.now + 0.5)
+
+    unfinished = [2, 2]
+
+    def then(t, stream, follow):
+        yield from stream
+        unfinished[t] -= 1
+        if unfinished[t] == 0:
+            net.spawn(follow)
+
+    image_tower = tower(0, image_out, [[stream_b(k) for k in range(B_STREAMS - 1)]])
+    text_tower = tower(
+        1, text_out, [[stream_a(k) for k in range(A_STREAMS)], [stream_b(B_STREAMS - 1)]]
+    )
+    for k in range(2):
+        stream = image_reduce(k)
+        net.spawn(then(0, stream, image_tower), next(stream))
+    image_pair = (s["image_hi"][...], s["image_lo"][...])
+    grad_pair = (s["pair_hi"][...], s["pair_lo"][...])
+    s["text_sum"][...] = (logit_scale * dot3(grad_pair, image_pair, ((0,), (0,)))).reshape(
+        2, NY, NX, 2, 8, width
+    )
+    net.now += 3.0
+    net.spawn(then(1, text_reduce(0, "y", "x", (NY, NX)), text_tower))
+    net.spawn(then(1, text_reduce(1, "x", "y", (NX, NY)), text_tower))
+    interleave(net, [])
     net.finish()
 
 
@@ -521,6 +585,24 @@
     same_a = (i == a) & (a >= 0) & (a < half)
     same_b = (i == b) & (b >= half) & (b < rows)
     return jnp.where(same_a | same_b, 1.0, 0.0)
+
+
+def leave_kernel(image, text, total, image_out, text_out, first, second, semaphores):
+    count = first.shape[0]
+    third = count // 3
+    copies = [(image, image_out), (text, text_out)]
+    for t, out in ((0, first), (1, second)):
+        for k in range(3):
+            copies.append(
+                (total.at[pl.ds(t * count + k * third, third)], out.at[pl.ds(k * third, third)])
+            )
+    copies = [
+        pltpu.make_async_copy(src, dst, semaphores.at[k]) for k, (src, dst) in enumerate(copies)
+    ]
+    for one in copies:
+        one.start()
+    for one in copies:
+        one.wait()
 
 
 def on_device(image_features, text_features, image_proj, text_proj):
@@ -544,9 +626,23 @@
             collective_id=1, has_side_effects=True, vmem_limit_bytes=60 * 2**20
         ),
     )(image_features, text_features, image_proj.T, text_proj.T)
-    weights = total.reshape(2, part // 8, width // 128, 8, 128).transpose(0, 1, 3, 2, 4)
-    weights = weights.reshape(2, part, width)
-    return (grad_image, grad_text, weights[0].T, weights[1].T)
+    half_shape = (part // 8 * (width // 128), 8, 128)
+    grad_image, grad_text, first, second = pl.pallas_call(
+        leave_kernel,
+        out_shape=[
+            jax.ShapeDtypeStruct(shape, jnp.float32)
+            for shape in ((rows, width), (rows, width), half_shape, half_shape)
+        ],
+        in_specs=[vmem] * 3,
+        out_specs=[anywhere] * 4,
+        scratch_shapes=[pltpu.SemaphoreType.DMA((8,))],
+    )(grad_image, grad_text, total)
+
+    def untiled(tiles):
+        tiles = tiles.reshape(part // 8, width // 128, 8, 128).transpose(0, 2, 1, 3)
+        return tiles.reshape(part, width).T
+
+    return (grad_image, grad_text, untiled(first), untiled(second))
 
 
 def solution(mesh):

time: 152 us -> 148 us (0.974)
  local copies, waits for them, and re-layouts: 4.77 us -> 0 us
    pallas_call x0 -> x1, Pallas kernels: none -> 3.58 us  [on_device(): pl.pallas_call(leave_kernel, out_shape=[jax.ShapeDtypeStruct(shape, jnp.f...]
    transpose x1 -> x0, local copies, waits for them, and re-layouts: 3.44 us -> none  [on_device(): return (grad_image, grad_text, weights[0].T, weights[1].T)]
    pallas_call x1, Pallas kernels: 146 us -> 144 us  [on_device(): pl.pallas_call(functools.partial(kernel, tuple(shapes)), out_shape=[jax.S...]
where the time goes in v5:
time: 148 us
  Pallas kernels  147 us (99%)
    pallas_call x1, Pallas kernels, on_device(): pl.pallas_call(functools.partial(kernel, tuple(shapes)), out_shape=[jax.S...  144 us
    pallas_call x1, Pallas kernels, on_device(): pl.pallas_call(leave_kernel, out_shape=[jax.ShapeDtypeStruct(shape, jnp.f...  3.58 us

profile of v5, /device:TPU:8, one launch (start us, length us, event | category | flops | bytes accessed | tf_op | source)
XLA Modules:
  0.0 148.2 jit_solution(18164967563352570086)
XLA Ops:
  0.6 143.8 %shard_map.75 = (f32[32,1152]{1,0:T(8,128)}, f32[32,1152]{1,0:T(8,128)}, f32[648,8,128]{2,1,0:T(8,128)}) custom-call(f32[32,1152]{1,0:T(8,128)} %image_x.1, f32[32,1152]{1,0:T(8,128)} %text_x.1, f32[288,1152]{1,0:T(8,128)} %bitcast.16, f32[288,1152]{1,0:T(8,128)} %bitcast.17), custom_call_target="tpu_custom_call" | custom-call | tf_op jit(solution)/shard_map/pallas_call | solution.py:616
  144.4 3.6 %shard_map.76 = (f32[32,1152]{1,0:T(8,128)}, f32[32,1152]{1,0:T(8,128)}, f32[324,8,128]{2,1,0:T(8,128)}, f32[324,8,128]{2,1,0:T(8,128)}) custom-call(f32[32,1152]{1,0:T(8,128)} %get-tuple-element.11.image, f32[32,1152]{1,0:T(8,128)} %get-tuple-element.12.text, f32[648,8,128]{2,1,0:T(8,128)} %get-tuple-element.13.total), custom_call_target="tpu_custom_call" | custom-call | tf_op jit(solution)/shard_map/pallas_call | solution.py:630

commit v6 on v5

--- a/solution.py
+++ b/solution.py
@@ -15,7 +15,7 @@
 GROUP = ("xl", "core")
 MESH = pl.DeviceIdType.MESH
 COPIES = 320
-LINK_RATE, LINK_DELAY = 45e3, 2.0
+LINK_RATE, LINK_DELAY = 45e3, 3.2
 CORE_RATE, CORE_DELAY = 350e3, 1.0
 
 
@@ -180,9 +180,9 @@
     return one(a[0], b[0]) + (one(a[0], b[1]) + one(a[1], b[0]))
 
 
-A_STREAMS, B_STREAMS = 2, 2
+A_STREAMS, B_STREAMS = 3, 2
 AZ, AY = 16, 2
-BY, BZ = 49, 7
+BY, BZ = 33, 5
 B_TILES = B_STREAMS * NY * BY
 
 
@@ -303,7 +303,6 @@
     )
     net = Net(send, recv)
     (me, sib, far, diag), (to_sib, to_far, to_diag) = group_places(net)
-    partner = net.device(x=(net.x + 2) % NX)
     rows, width = image_x.shape
     part = image_w.shape[0]
 
@@ -519,7 +518,7 @@
 
     def stream_b(k):
         return weight_stream_b(
-            net, partner, k * NY * BY, terms, total,
+            net, net.device(x=(net.x + 2) % NX), k * NY * BY, terms, total,
             *pick("b%d" % k, "mid", "own", "pair", "every", "yl", "yr", "zl", "zr"),
         )
 
@@ -556,9 +555,9 @@
         if unfinished[t] == 0:
             net.spawn(follow)
 
-    image_tower = tower(0, image_out, [[stream_b(k) for k in range(B_STREAMS - 1)]])
+    image_tower = tower(0, image_out, [[stream_b(k) for k in range(B_STREAMS)]])
     text_tower = tower(
-        1, text_out, [[stream_a(k) for k in range(A_STREAMS)], [stream_b(B_STREAMS - 1)]]
+        1, text_out, [[stream_a(k) for k in range(A_STREAMS)]]
     )
     for k in range(2):
         stream = image_reduce(k)
@@ -587,21 +586,26 @@
     return jnp.where(same_a | same_b, 1.0, 0.0)
 
 
-def leave_kernel(image, text, total, image_out, text_out, first, second, semaphores):
+def leave_kernel(image, text, total, image_out, text_out, first, second,
+                 image_held, text_held, held, arrived, left):
     count = first.shape[0]
     third = count // 3
-    copies = [(image, image_out), (text, text_out)]
+    moves = []
     for t, out in ((0, first), (1, second)):
         for k in range(3):
-            copies.append(
-                (total.at[pl.ds(t * count + k * third, third)], out.at[pl.ds(k * third, third)])
-            )
-    copies = [
-        pltpu.make_async_copy(src, dst, semaphores.at[k]) for k, (src, dst) in enumerate(copies)
+            there, here = pl.ds(t * count + k * third, third), pl.ds(k * third, third)
+            moves.append((total.at[there], held.at[there], out.at[here]))
+    moves += [(image, image_held, image_out), (text, text_held, text_out)]
+    reads = [
+        pltpu.make_async_copy(src, mid, arrived.at[k]) for k, (src, mid, _) in enumerate(moves)
     ]
-    for one in copies:
+    writes = [pltpu.make_async_copy(mid, out, left.at[k]) for k, (_, mid, out) in enumerate(moves)]
+    for one in reads:
         one.start()
-    for one in copies:
+    for read, write in zip(reads, writes):
+        read.wait()
+        write.start()
+    for one in writes:
         one.wait()
 
 
@@ -612,6 +616,7 @@
     total_shape = (2 * part // 8 * (width // 128), 8, 128)
     vmem = pl.BlockSpec(memory_space=pltpu.VMEM)
     anywhere = pl.BlockSpec(memory_space=pl.ANY)
+    hbm = pl.BlockSpec(memory_space=pltpu.HBM)
     semaphores = [pltpu.SemaphoreType.DMA((n,)) for n in (COPIES, COPIES, 2)]
     grad_image, grad_text, total = pl.pallas_call(
         functools.partial(kernel, tuple(shapes)),
@@ -633,9 +638,12 @@
             jax.ShapeDtypeStruct(shape, jnp.float32)
             for shape in ((rows, width), (rows, width), half_shape, half_shape)
         ],
-        in_specs=[vmem] * 3,
-        out_specs=[anywhere] * 4,
-        scratch_shapes=[pltpu.SemaphoreType.DMA((8,))],
+        in_specs=[hbm] * 3,
+        out_specs=[hbm] * 4,
+        scratch_shapes=[
+            pltpu.VMEM(shape, jnp.float32) for shape in ((rows, width), (rows, width), total_shape)
+        ]
+        + [pltpu.SemaphoreType.DMA((8,))] * 2,
     )(grad_image, grad_text, total)
 
     def untiled(tiles):

time: 148 us -> 144 us (0.973)
  Pallas kernels: 147 us -> 143 us
    pallas_call x1, Pallas kernels: 144 us -> 140 us  [on_device(): pl.pallas_call(functools.partial(kernel, tuple(shapes)), out_shape=[jax.S...]
where the time goes in v6:
time: 144 us
  Pallas kernels  143 us (99%)
    pallas_call x1, Pallas kernels, on_device(): pl.pallas_call(functools.partial(kernel, tuple(shapes)), out_shape=[jax.S...  140 us

profile of v6, /device:TPU:8, one launch (start us, length us, event | category | flops | bytes accessed | tf_op | source)
XLA Modules:
  0.0 144.0 jit_solution(8111974674352068394)
XLA Ops:
  0.6 140.4 %shard_map.75 = (f32[32,1152]{1,0:T(8,128)}, f32[32,1152]{1,0:T(8,128)}, f32[648,8,128]{2,1,0:T(8,128)}) custom-call(f32[32,1152]{1,0:T(8,128)} %image_x.1, f32[32,1152]{1,0:T(8,128)} %text_x.1, f32[288,1152]{1,0:T(8,128)} %bitcast.16, f32[288,1152]{1,0:T(8,128)} %bitcast.17), custom_call_target="tpu_custom_call" | custom-call | tf_op jit(solution)/shard_map/pallas_call | solution.py:621
  141.1 2.7 %shard_map.76 = (f32[32,1152]{1,0:T(8,128)}, f32[32,1152]{1,0:T(8,128)}, f32[324,8,128]{2,1,0:T(8,128)}, f32[324,8,128]{2,1,0:T(8,128)}) custom-call(f32[32,1152]{1,0:T(8,128)} %get-tuple-element.11.image, f32[32,1152]{1,0:T(8,128)} %get-tuple-element.12.text, f32[648,8,128]{2,1,0:T(8,128)} %get-tuple-element.13.total), custom_call_target="tpu_custom_call" | custom-call | tf_op jit(solution)/shard_map/pallas_call | solution.py:635

commit v7 on v6

--- a/solution.py
+++ b/solution.py
@@ -524,9 +524,8 @@
 
     def in_turn(streams):
         for stream in streams:
-            due = next(stream)
-            net.spawn(stream, due)
-            yield due
+            net.spawn(stream, next(stream))
+        yield net.now
 
     def tower(t, out, streams):
         g, u = s["grad"][t].reshape(rows, width), unit[t]

time: 144 us -> 144 us (level)
  no operation moved by 1% of the time
where the time goes in v7:
time: 144 us
  Pallas kernels  143 us (99%)
    pallas_call x1, Pallas kernels, on_device(): pl.pallas_call(functools.partial(kernel, tuple(shapes)), out_shape=[jax.S...  141 us

profile of v7, /device:TPU:8, one launch (start us, length us, event | category | flops | bytes accessed | tf_op | source)
XLA Modules:
  0.0 144.1 jit_solution(10455062217709582690)
XLA Ops:
  0.6 140.6 %shard_map.75 = (f32[32,1152]{1,0:T(8,128)}, f32[32,1152]{1,0:T(8,128)}, f32[648,8,128]{2,1,0:T(8,128)}) custom-call(f32[32,1152]{1,0:T(8,128)} %image_x.1, f32[32,1152]{1,0:T(8,128)} %text_x.1, f32[288,1152]{1,0:T(8,128)} %bitcast.16, f32[288,1152]{1,0:T(8,128)} %bitcast.17), custom_call_target="tpu_custom_call" | custom-call | tf_op jit(solution)/shard_map/pallas_call | solution.py:620
  141.2 2.7 %shard_map.76 = (f32[32,1152]{1,0:T(8,128)}, f32[32,1152]{1,0:T(8,128)}, f32[324,8,128]{2,1,0:T(8,128)}, f32[324,8,128]{2,1,0:T(8,128)}) custom-call(f32[32,1152]{1,0:T(8,128)} %get-tuple-element.11.image, f32[32,1152]{1,0:T(8,128)} %get-tuple-element.12.text, f32[648,8,128]{2,1,0:T(8,128)} %get-tuple-element.13.total), custom_call_target="tpu_custom_call" | custom-call | tf_op jit(solution)/shard_map/pallas_call | solution.py:634
